TPU v7x, 128 devices: a whole 4x4x4 slice. The times are simulated.
128 devices in a mesh: item: 16 (over y, x_lo, core), center: 8 (over x_hi, z).
Axes of the slice: x: 4 (x_hi: 2, x_lo: 2; x = x_hi * 2 + x_lo), y: 4, z: 4, core: 2. Of those that a mesh axis runs over, the one named last changes fastest.
Arguments:
- embeddings: bfloat16 [32768, 512], P('item'), may hold values from -6 to 6
- codes: int32 [3, 32768], P(None, 'item'), may hold values from 0 to 16383, as said below
- codebooks: bfloat16 [3, 16384, 512], P(None, 'center'), may hold values from -6 to 6
Outputs:
- new_codebooks: bfloat16 [3, 16384, 512], P(None, 'center')
- final_residual: bfloat16 [32768, 512], P('item')
Inputs may be any that keep to these rules, and one draw needn't show every extreme that they name: At every level, of the 2048 items of one group of consecutive items at most 32 have codes in any one aligned block of 128 consecutive centers, and in every group some block holds exactly 32.
All inputs are finite; a program needn't handle non-finite values.
Results may differ from a plain program's by a relative error of at most 0.018.
Values may be sent and summed in bfloat16 or wider, within the bound.
A program may use at most 128 MiB of HBM per device.

v0:
```python
import jax
import jax.numpy as jnp
from jax import lax
from jax.sharding import PartitionSpec as P

prior_weight = 1.0


def per_device(embeddings, codes, codebooks):
    shard_size = codebooks.shape[1]
    center_base = lax.axis_index("center") * shard_size
    labels = center_base + lax.broadcasted_iota(jnp.int32, (1, shard_size), 1)
    residual = embeddings
    new_books = []
    for level_index in range(codebooks.shape[0]):
        member = codes[level_index][:, None] == labels
        onehot = member.astype(jnp.bfloat16)
        previous = codebooks[level_index]
        pooled = lax.dot_general(
            onehot, residual, (((0,), (0,)), ((), ())), preferred_element_type=jnp.float32
        )
        counts = jnp.sum(member.astype(jnp.float32), axis=0)
        summed, number = (
            lax.psum(pooled.astype(jnp.bfloat16), "item").astype(jnp.float32),
            lax.psum(counts.astype(jnp.bfloat16), "item").astype(jnp.float32),
        )
        updated = (
            (summed + prior_weight * previous.astype(jnp.float32))
            / (number[:, None] + prior_weight)
        ).astype(jnp.bfloat16)
        new_books.append(updated)
        assigned = jnp.dot(onehot, updated, preferred_element_type=jnp.float32)
        assigned = lax.psum(assigned.astype(jnp.bfloat16), "center").astype(jnp.float32)
        residual = (residual.astype(jnp.float32) - assigned).astype(jnp.bfloat16)
    return (jnp.stack(new_books), residual)


def solution(mesh):
    placed = (P("item", None), P(None, "item"), P(None, "center", None))
    return jax.shard_map(
        per_device,
        mesh=mesh,
        in_specs=placed,
        out_specs=(P(None, "center", None), P("item", None)),
        check_vma=False,
    )
```

profile of v0, /device:TPU:0, one launch (start us, length us, event | category | flops | bytes accessed | tf_op | source)
XLA Modules:
  0.0 729.7 jit_solution(5812779327244110795)
XLA Ops:
  7.2 0.0 all-reduce.8.cloned.1.call-start
  7.2 0.9 fusion.51
  8.1 8.2 %fusion.33 = bf16[2048,512]{1,0:T(8,128)(2,1)} fusion(bf16[2048,512]{1,0:T(8,128)(2,1)} %param.3, s32[2048]{0:T(1024)S(1)} %iota_add_fusion, s32[2048]{0:T(1024)S(1)} %bitcast.28), kind=kOutput, calls=%fused_computation.43 | convolution fusion | flops 4300210176 | bytes 4210688 | tf_op jit(solution)/shard_map/dot_general | solution.py:19
  16.3 0.0 all-reduce.8.cloned.1.call-update
  16.3 0.0 all-reduce.10.cloned.1.call-start
  16.4 5.9 fusion.14
  22.3 56.3 %all-reduce = (bf16[2048]{0:T(1024)(128)(2,1)S(1)}, bf16[2048]{0:T(1024)(128)(2,1)S(1)}, bf16[2048]{0:T(1024)(128)(2,1)S(1)}) all-reduce(bf16[2048]{0:T(1024)(128)(2,1)S(1)} %get-tuple-element.4, bf16[2048]{0:T(1024)(128)(2,1)S(1)} %get-tuple-element.3, ...), channel_id=1, replica_groups=mesh['item'=16,'center'=8] {'item'}, use_global_device_ids=true, to_apply=%region_2.0 | all-reduce | flops 6144 | bytes 24576 | tf_op jit(solution)/shard_map/psum | solution.py:25
  78.5 65.7 %all-reduce.8.cloned.1.call-done = bf16[2048,512]{1,0:T(8,128)(2,1)} async-done(((bf16[2048,512]{1,0:T(8,128)(2,1)}), bf16[2048,512]{1,0:T(8,128)(2,1)}) %all-reduce.8.cloned.1.call-update) | async-done | bytes 2097168 | tf_op jit(solution)/shard_map/psum | solution.py:24
  144.2 2.5 fusion.32
  146.8 5.8 fusion.36
  152.5 0.2 all-reduce.12.cloned.1.call-start
  152.8 92.5 %all-reduce.10.cloned.1.call-done = bf16[2048,512]{1,0:T(8,128)(2,1)} async-done(((bf16[2048,512]{1,0:T(8,128)(2,1)}), bf16[2048,512]{1,0:T(8,128)(2,1)}) %all-reduce.10.cloned.1.call-update) | async-done | bytes 2097168 | tf_op jit(solution)/shard_map/psum | solution.py:33
  245.3 8.9 %fusion.39 = bf16[2048,512]{1,0:T(8,128)(2,1)} fusion(s32[2048]{0:T(1024)S(1)} %iota_add_fusion, s32[2048]{0:T(1024)S(1)} %bitcast.26, bf16[2048,512]{1,0:T(8,128)(2,1)} %all-reduce.10.cloned.1.call-done, bf16[2048,512]{1,0:T(8,128)(2,1)} %param.3), kind=kOutput, calls=%fused_computation.45 | convolution fusion | flops 4304404480 | bytes 6307840 | tf_op jit(solution)/shard_map/dot_general | solution.py:19
  254.2 0.0 all-reduce.12.cloned.1.call-update
  254.2 0.0 all-reduce.14.cloned.1.call-start
  254.2 124.1 %all-reduce.12.cloned.1.call-done = bf16[2048,512]{1,0:T(8,128)(2,1)} async-done(((bf16[2048,512]{1,0:T(8,128)(2,1)}), bf16[2048,512]{1,0:T(8,128)(2,1)}) %all-reduce.12.cloned.1.call-update) | async-done | bytes 2097168 | tf_op jit(solution)/shard_map/psum | solution.py:24
  378.4 2.5 fusion.30
  380.9 1.3 copy-done
  382.3 5.7 fusion.42
  388.0 0.0 all-reduce.14.cloned.1.call-update
  388.0 0.3 all-reduce.16.cloned.1.call-start
  388.3 92.6 %all-reduce.14.cloned.1.call-done = bf16[2048,512]{1,0:T(8,128)(2,1)} async-done(((bf16[2048,512]{1,0:T(8,128)(2,1)}), bf16[2048,512]{1,0:T(8,128)(2,1)}) %all-reduce.14.cloned.1.call-update) | async-done | bytes 2097168 | tf_op jit(solution)/shard_map/psum | solution.py:33
  480.9 9.5 %fusion.45 = bf16[2048,512]{1,0:T(8,128)(2,1)} fusion(s32[2048]{0:T(1024)S(1)} %iota_add_fusion, s32[2048]{0:T(1024)S(1)} %bitcast.23, bf16[2048,512]{1,0:T(8,128)(2,1)} %all-reduce.14.cloned.1.call-done, bf16[2048,512]{1,0:T(8,128)(2,1)} %all-reduce.10.cloned.1.call-done, bf16[2048,512]{1,0:T(8,128)(2,1)} %param.3), kind=kOutput, calls=%fused_computation.47 | convolution fusion | flops 4308598784 | bytes 8404992 | tf_op jit(solution)/shard_map/dot_general | solution.py:19
  490.4 0.0 all-reduce.16.cloned.1.call-update
  490.4 0.0 all-reduce.18.cloned.1.call-start
  490.5 124.1 %all-reduce.16.cloned.1.call-done = bf16[2048,512]{1,0:T(8,128)(2,1)} async-done(((bf16[2048,512]{1,0:T(8,128)(2,1)}), bf16[2048,512]{1,0:T(8,128)(2,1)}) %all-reduce.16.cloned.1.call-update) | async-done | bytes 2097168 | tf_op jit(solution)/shard_map/psum | solution.py:24
  614.6 2.5 fusion.28
  617.1 1.3 copy-done.1
  618.4 5.7 fusion.48
  624.2 5.5 pad_maximum_fusion
  629.7 87.3 %all-reduce.18.cloned.1.call-done = bf16[2048,512]{1,0:T(8,128)(2,1)} async-done(((bf16[2048,512]{1,0:T(8,128)(2,1)}), bf16[2048,512]{1,0:T(8,128)(2,1)}) %all-reduce.18.cloned.1.call-update) | async-done | bytes 2097168 | tf_op jit(solution)/shard_map/psum | solution.py:33
  716.9 5.9 subtract_convert_fusion
  (8 shorter events, 0.1 us)
Async XLA Ops:
  7.2 137.1 %all-reduce.8.cloned.1.call-start = ((), (), s32[]{:S(2)}) async-start(), calls=%async_computation | async-start | bytes 4194304 | tf_op jit(solution)/shard_map/psum | solution.py:24
  16.3 229.0 %all-reduce.10.cloned.1.call-start = ((), (), s32[]{:S(2)}) async-start(), calls=%async_computation.1 | async-start | bytes 4194304 | tf_op jit(solution)/shard_map/psum | solution.py:33
  152.5 225.8 %all-reduce.12.cloned.1.call-start = ((), (), s32[]{:S(2)}) async-start(), calls=%async_computation.2 | async-start | bytes 4194304 | tf_op jit(solution)/shard_map/psum | solution.py:24
  254.2 226.7 %all-reduce.14.cloned.1.call-start = ((), (), s32[]{:S(2)}) async-start(), calls=%async_computation.3 | async-start | bytes 4194304 | tf_op jit(solution)/shard_map/psum | solution.py:33
  380.9 1.3 copy-start
  388.0 226.5 %all-reduce.16.cloned.1.call-start = ((), (), s32[]{:S(2)}) async-start(), calls=%async_computation.4 | async-start | bytes 4194304 | tf_op jit(solution)/shard_map/psum | solution.py:24
  490.4 226.6 %all-reduce.18.cloned.1.call-start = ((), (), s32[]{:S(2)}) async-start(), calls=%async_computation.5 | async-start | bytes 4194304 | tf_op jit(solution)/shard_map/psum | solution.py:33
  617.1 1.3 copy-start.1
Sparse Core Ops, SparseCore 0:
  16.5 127.7 all-reduce.7
  152.7 92.5 all-reduce.9
  254.3 124.0 all-reduce.11
  388.1 92.6 all-reduce.13
  490.5 124.0 all-reduce.15
  624.3 92.5 all-reduce.17
where the time goes:
time: 730 us
  waiting for transfers between devices  586 us (80%)
  blocking collectives  56.3 us (8%)
  matrix products  43.8 us (6%)
  other arithmetic  24.9 us (3%)
  between operations  14.2 us (2%)
    psum x3, waiting for transfers between devices, per_device(): lax.psum(pooled.astype(jnp.bfloat16), 'item').astype(jnp.float32)  314 us
    psum x3, waiting for transfers between devices, per_device(): lax.psum(assigned.astype(jnp.bfloat16), 'center').astype(jnp.float32)  272 us
    psum x1, blocking collectives, per_device(): lax.psum(counts.astype(jnp.bfloat16), 'item').astype(jnp.float32)  56.3 us
    dot_general x3, matrix products, per_device(): lax.dot_general(onehot, residual, (((0,), (0,)), ((), ())), preferred_ele...  26.6 us
    dot_general x3, matrix products, per_device(): assigned = jnp.dot(onehot, updated, preferred_element_type=jnp.float32)  17.2 us
  transfers between devices with their start and end apart: 6, of which 6 were waited for; matrix products, arithmetic and copies ran while one was open for 2% of the time, Pallas kernels for 0%

commit v1 on v0

v1 whole, which is shorter than its diff:
```python
import functools

import jax
import jax.numpy as jnp
from jax import lax
from jax.experimental import pallas as pl
from jax.experimental.pallas import tpu as pltpu
from jax.sharding import PartitionSpec as P

MESH = pl.DeviceIdType.MESH
LEVELS, ITEMS, DIM = 3, 2048, 512
N_ITEM, N_CENTER, SHARE, CAP = 16, 8, 128, 32
SLOTS = N_ITEM * CAP
HOP1, HOP2, HOME = 64, 80, ITEMS // N_CENTER
LANES = 128
F32, BF16, I32 = jnp.float32, jnp.bfloat16, jnp.int32


def iota(shape, axis):
    return lax.broadcasted_iota(I32, shape, axis)


def onehot(match):
    return match.astype(F32).astype(BF16)


def dot(a, b):
    return jnp.dot(a, b, preferred_element_type=F32)


ROW_SLOT0 = 0
ROW_OFF = 16
ROW_D1 = 28
ROW_D2 = 40
ROW_D3 = 52
ROW_POS = 64
ROWS = 80


def prep_kernel(codes_ref, out_ref):
    me = lax.axis_index("center")
    a, b = iota((LANES, 2 * LANES), 0), iota((LANES, 2 * LANES), 1)
    before = onehot((b >= LANES) | (a < b))

    def ordered(cls, n_cls, lower=None):
        member = onehot(iota((n_cls, ITEMS), 0) == cls)
        seen = jnp.zeros((n_cls, LANES), F32)
        ranks = []
        for k in range(ITEMS // LANES):
            part = member[:, k * LANES : (k + 1) * LANES]
            both = dot(part, before)
            ranks.append(jnp.sum(part.astype(F32) * (both[:, :LANES] + seen), axis=0, keepdims=True))
            seen = seen + both[:, LANES:]
        rank = jnp.concatenate(ranks, axis=1).astype(I32)
        if lower is None:
            return rank, None
        r, s = iota((n_cls, n_cls), 0), iota((n_cls, n_cls), 1)
        start = jnp.dot(lower(r, s).astype(F32), seen, precision=lax.Precision.HIGHEST, preferred_element_type=F32)
        start = jnp.concatenate([start] * (ITEMS // LANES), axis=1)
        return rank, jnp.sum(member.astype(F32) * start, axis=0, keepdims=True).astype(I32)

    def extract(pos, n_pos, attrs):
        n_hi = n_pos // LANES
        low = onehot(iota((LANES, ITEMS), 0) == jnp.where(pos >= 0, pos % LANES, -1))
        high = iota((8, ITEMS), 0) == jnp.where(pos >= 0, pos // LANES, -1)
        rows = jnp.concatenate([jnp.where(high, at, 0) for at in attrs], axis=0).astype(F32).astype(BF16)
        got = lax.dot_general(rows, low, (((1,), (1,)), ((), ())), preferred_element_type=F32).astype(I32)
        return [got[8 * k : 8 * k + n_hi] for k in range(len(attrs))]

    out_ref[...] = jnp.zeros_like(out_ref)
    shard, off, local = [], [], []
    for lev in range(LEVELS):
        code = codes_ref[lev : lev + 1, :]
        block = code // SHARE
        rank, _ = ordered(block, N_ITEM * N_CENTER)
        slot = (block % N_ITEM) * CAP + rank
        shard.append(code // (SHARE * N_ITEM))
        off.append(code % SHARE)
        local.append(jnp.where(shard[lev] == me, slot, -1))
    for k in range(ITEMS // LANES):
        out_ref[ROW_SLOT0 + k : ROW_SLOT0 + k + 1, :] = local[0][:, k * LANES : (k + 1) * LANES]

    for lev in range(LEVELS):
        here = shard[lev]
        if lev < LEVELS - 1:
            there = shard[lev + 1]
            rank, start = ordered(
                here * N_CENTER + there, N_CENTER * N_CENTER, lambda r, s: (r // N_CENTER == s // N_CENTER) & (s < r)
            )
            order = rank + start
            via, place = order % N_CENTER, order // N_CENTER
            second, _ = ordered(via * N_CENTER + there, N_CENTER * N_CENTER)
            target = [there + 1, second]
            base = HOP2
            pos3 = jnp.where(there == me, via * HOP2 + second, -1)
            slot_next = local[lev + 1]
            hi3, lo3 = extract(pos3, N_CENTER * HOP2, [jnp.maximum(slot_next, 0) // 256 + 1, jnp.maximum(slot_next, 0) % 256])
            d3 = (hi3 - 1) * 256 + lo3
            out_ref[ROW_D3 + 6 * lev : ROW_D3 + 6 * lev + 5, :] = d3
        else:
            rank, start = ordered(here, N_CENTER, lambda r, s: s < r)
            order = rank + start
            via, place = order % N_CENTER, rank // N_CENTER
            target = [jnp.ones_like(order), order // N_CENTER]
            base = HOME
            for k in range(ITEMS // LANES):
                out_ref[ROW_POS + k : ROW_POS + k + 1, :] = (via * HOME + order // N_CENTER)[:, k * LANES : (k + 1) * LANES]
        off_s, via_s, place_s = extract(local[lev], SLOTS, [off[lev] + 1, via + 1, place])
        out_ref[ROW_OFF + 4 * lev : ROW_OFF + 4 * lev + 4, :] = off_s
        out_ref[ROW_D1 + 4 * lev : ROW_D1 + 4 * lev + 4, :] = (via_s - 1) * HOP1 + place_s
        pos2 = jnp.where(via == me, here * HOP1 + place, -1)
        hi2, lo2 = extract(pos2, N_CENTER * HOP1, target)
        out_ref[ROW_D2 + 4 * lev : ROW_D2 + 4 * lev + 4, :] = (hi2 - 1) * base + lo2


ITEM_OFFSETS = [(y, x, c) for y in range(4) for x in range(2) for c in range(2)][1:]
CHIP_OFFSETS = [o for o in ITEM_OFFSETS if o[2] == 0]
CENTER_OFFSETS = [(h, z) for h in range(2) for z in range(4)][1:]


def main_kernel(
    idx_ref, emb_ref, cb_ref, books_ref, final_ref,
    cb, meta_s, meta_r, dsend, drecv, book, nres, h1s, h1r, h2s, h2r, fsend, frecv, scatter, poscol,
    cb_sem, meta_ss, meta_rs, d_ss, d_rs, g_ss, g_rs, p_ss, p_rs, h1_ss, h1_rs, h2_ss, h2_rs, f_ss, f_rs, out_sem,
):
    item, center = lax.axis_index("item"), lax.axis_index("center")
    my_y, my_x, my_c = item // 4, (item // 2) % 2, item % 2
    my_h, my_z = center // 4, center % 4

    def item_at(o):
        return ((my_y + o[0]) % 4) * 4 + ((my_x + o[1]) % 2) * 2 + (my_c + o[2]) % 2

    def item_from(o):
        return ((my_y + 4 - o[0]) % 4) * 4 + ((my_x + o[1]) % 2) * 2 + (my_c + o[2]) % 2

    def center_at(o):
        return ((my_h + o[0]) % 2) * 4 + (my_z + o[1]) % 4

    def rows(start, size, step):
        return pl.ds(pl.multiple_of(start * step, step), size)

    barrier = pltpu.get_barrier_semaphore()
    for o in ITEM_OFFSETS:
        pl.semaphore_signal(barrier, inc=1, device_id=(item_at(o), center), device_id_type=MESH)
    for o in CENTER_OFFSETS:
        pl.semaphore_signal(barrier, inc=1, device_id=(item, center_at(o)), device_id_type=MESH)

    own_cb = pltpu.make_async_copy(cb_ref.at[:, rows(item, SHARE, SHARE), :], cb, cb_sem)
    own_cb.start()

    sends = []

    def send(src, dst, ss, rs, to):
        cp = pltpu.make_async_remote_copy(
            src_ref=src, dst_ref=dst, send_sem=ss, recv_sem=rs, device_id=to, device_id_type=MESH
        )
        cp.start()
        sends.append(cp)
        return cp

    meta_s[...] = jnp.zeros_like(meta_s)
    for h in range(4):
        for lev in range(LEVELS):
            meta_s[h, lev : lev + 1, :] = idx_ref[ROW_OFF + 4 * lev + h : ROW_OFF + 4 * lev + h + 1, :]

    for k in range(ITEMS // LANES):
        row = idx_ref[ROW_SLOT0 + k : ROW_SLOT0 + k + 1, :]
        scatter[0:SLOTS, k * LANES : (k + 1) * LANES] = onehot(iota((SLOTS, LANES), 0) == row)
    dsend[0] = dot(scatter[0:SLOTS, :], emb_ref[...]).astype(BF16)

    pl.semaphore_wait(barrier, len(ITEM_OFFSETS) + len(CENTER_OFFSETS))

    metas = []
    for n, o in enumerate(ITEM_OFFSETS):
        to = item_at(o)
        metas.append(
            send(meta_s.at[to // 4], meta_r.at[item], meta_ss.at[n], meta_rs.at[n], (to, center))
        )
    meta_r[item] = meta_s[item // 4]

    def permute(first, n_in, n_out, source, out_dtype=BF16):
        parts = [
            onehot(iota((n_out, LANES), 0) == idx_ref[first + k : first + k + 1, :]) for k in range(n_in // LANES)
        ]
        return dot(jnp.concatenate(parts, axis=1), source).astype(out_dtype)

    own_rows = rows(item, CAP, CAP)
    own_block = rows(item, SHARE, SHARE)
    metas_done = False
    for lev in range(LEVELS):
        cps = []
        for n, o in enumerate(ITEM_OFFSETS):
            to = item_at(o)
            cps.append(
                send(dsend.at[lev, rows(to, CAP, CAP)], drecv.at[lev, own_rows], d_ss.at[lev, n], d_rs.at[lev, n], (to, center))
            )
        drecv[lev, own_rows, :] = dsend[lev, own_rows, :]
        if not metas_done:
            for cp in metas:
                cp.wait_recv()
            own_cb.wait()
            metas_done = True
        members = []
        lane = iota((8, LANES), 1)
        mine = (lane >= (item % 4) * CAP) & (lane < (item % 4 + 1) * CAP)
        for q in range(4):
            total = jnp.zeros((8, LANES), I32)
            for j in range(4):
                piece = jnp.where(mine, meta_r[4 * q + j], 0)
                total = total + pltpu.roll(piece, ((j + 4 - item % 4) % 4) * CAP, 1)
            members.append((iota((SHARE, LANES), 0) + 1 == total[lev : lev + 1, :]).astype(F32))
        member = jnp.concatenate(members, axis=1)
        count = jnp.sum(member, axis=1, keepdims=True)
        for cp in cps:
            cp.wait_recv()
        pooled = dot(member.astype(BF16), drecv[lev])
        updated = ((pooled + cb[lev].astype(F32)) / (count + 1.0)).astype(BF16)
        book[lev, own_block, :] = updated
        cps = []
        for n, o in enumerate(CHIP_OFFSETS):
            to = item_at(o)
            cps.append(
                send(book.at[lev, own_block], book.at[lev, own_block], g_ss.at[lev, n], g_rs.at[lev, n], (to, center))
            )
        partner = (item_at((0, 0, 1)), center)
        forwards = [send(book.at[lev, own_block], book.at[lev, own_block], p_ss.at[lev, 7], p_rs.at[lev, 7], partner)]
        assigns = []
        for h in range(4):
            row = idx_ref[ROW_OFF + 4 * lev + h : ROW_OFF + 4 * lev + h + 1, :]
            assigns.append((iota((SHARE, LANES), 0) + 1 == row).astype(F32).T.astype(BF16))
        for n, o in enumerate(CHIP_OFFSETS):
            cps[n].wait_recv()
            theirs = rows(item_from(o), SHARE, SHARE)
            forwards.append(send(book.at[lev, theirs], book.at[lev, theirs], p_ss.at[lev, n], p_rs.at[lev, n], partner))
        for cp in forwards:
            cp.wait_recv()
        out = pltpu.make_async_copy(book.at[lev], books_ref.at[lev], out_sem.at[lev])
        out.start()
        for b in range(N_ITEM):
            assigned = dot(assigns[b // 4][(b % 4) * CAP : (b % 4 + 1) * CAP, :], book[lev, b * SHARE : (b + 1) * SHARE, :])
            slots = slice(b * CAP, (b + 1) * CAP)
            nres[slots, :] = (dsend[lev, slots, :].astype(F32) - assigned.astype(BF16).astype(F32)).astype(BF16)
        h1s[lev] = permute(ROW_D1 + 4 * lev, SLOTS, N_CENTER * HOP1, nres[...])
        own = rows(center, HOP1, HOP1)
        cps = []
        for n, o in enumerate(CENTER_OFFSETS):
            to = center_at(o)
            cps.append(send(h1s.at[lev, rows(to, HOP1, HOP1)], h1r.at[lev, own], h1_ss.at[lev, n], h1_rs.at[lev, n], (item, to)))
        h1r[lev, own, :] = h1s[lev, own, :]
        for cp in cps:
            cp.wait_recv()
        if lev < LEVELS - 1:
            h2s[lev] = permute(ROW_D2 + 4 * lev, N_CENTER * HOP1, N_CENTER * HOP2, h1r[lev])
            own = rows(center, HOP2, HOP2)
            cps = []
            for n, o in enumerate(CENTER_OFFSETS):
                to = center_at(o)
                cps.append(send(h2s.at[lev, rows(to, HOP2, HOP2)], h2r.at[lev, own], h2_ss.at[lev, n], h2_rs.at[lev, n], (item, to)))
            h2r[lev, own, :] = h2s[lev, own, :]
            for cp in cps:
                cp.wait_recv()
            dsend[lev + 1] = permute(ROW_D3 + 6 * lev, N_CENTER * HOP2, SLOTS, h2r[lev])
        else:
            own = rows(center, HOME, HOME)
            frecv[own, :] = permute(ROW_D2 + 4 * lev, N_CENTER * HOP1, HOME, h1r[lev])
            cps = []
            for n, o in enumerate(CENTER_OFFSETS):
                cps.append(send(frecv.at[own], frecv.at[own], f_ss.at[n], f_rs.at[n], (item, center_at(o))))
            for k in range(ITEMS // LANES):
                row = jnp.broadcast_to(idx_ref[ROW_POS + k : ROW_POS + k + 1, :].astype(F32), (LANES, LANES))
                col = row.T.astype(I32)
                for g in range(ITEMS // LANES):
                    scatter[k * LANES : (k + 1) * LANES, g * LANES : (g + 1) * LANES] = onehot(iota((LANES, LANES), 1) + g * LANES == col)
            for cp in cps:
                cp.wait_recv()
            for k in range(ITEMS // 256):
                final_ref[k * 256 : (k + 1) * 256, :] = dot(scatter[k * 256 : (k + 1) * 256, :], frecv[...]).astype(BF16)
    for lev in range(LEVELS):
        pltpu.make_async_copy(book.at[lev], books_ref.at[lev], out_sem.at[lev]).wait()
    for cp in sends:
        cp.wait_send()


def per_device(embeddings, codes, codebooks):
    vmem = pl.BlockSpec(memory_space=pltpu.VMEM)
    hbm = pl.BlockSpec(memory_space=pl.ANY)
    idx = pl.pallas_call(
        prep_kernel,
        out_shape=jax.ShapeDtypeStruct((ROWS, LANES), I32),
        in_specs=[vmem],
        out_specs=vmem,
        compiler_params=pltpu.CompilerParams(vmem_limit_bytes=48 << 20),
    )(codes)
    dma = pltpu.SemaphoreType.DMA
    return pl.pallas_call(
        main_kernel,
        out_shape=(
            jax.ShapeDtypeStruct(codebooks.shape, BF16),
            jax.ShapeDtypeStruct(embeddings.shape, BF16),
        ),
        in_specs=[vmem, vmem, hbm],
        out_specs=(hbm, vmem),
        scratch_shapes=[
            pltpu.VMEM((LEVELS, SHARE, DIM), BF16),
            pltpu.VMEM((4, 8, LANES), I32),
            pltpu.VMEM((N_ITEM, 8, LANES), I32),
            pltpu.VMEM((LEVELS, SLOTS, DIM), BF16),
            pltpu.VMEM((LEVELS, SLOTS, DIM), BF16),
            pltpu.VMEM((LEVELS, N_ITEM * SHARE, DIM), BF16),
            pltpu.VMEM((SLOTS, DIM), BF16),
            pltpu.VMEM((LEVELS, N_CENTER * HOP1, DIM), BF16),
            pltpu.VMEM((LEVELS, N_CENTER * HOP1, DIM), BF16),
            pltpu.VMEM((LEVELS - 1, N_CENTER * HOP2, DIM), BF16),
            pltpu.VMEM((LEVELS - 1, N_CENTER * HOP2, DIM), BF16),
            pltpu.VMEM((8, LANES), F32),
            pltpu.VMEM((ITEMS, DIM), BF16),
            pltpu.VMEM((ITEMS, ITEMS), BF16),
            pltpu.VMEM((8, LANES), F32),
            dma,
            dma((15,)), dma((15,)),
            dma((LEVELS, 15)), dma((LEVELS, 15)),
            dma((LEVELS, 7)), dma((LEVELS, 7)),
            dma((LEVELS, 8)), dma((LEVELS, 8)),
            dma((LEVELS, 7)), dma((LEVELS, 7)),
            dma((LEVELS, 7)), dma((LEVELS, 7)),
            dma((7,)), dma((7,)),
            dma((LEVELS,)),
        ],
        compiler_params=pltpu.CompilerParams(collective_id=0, has_side_effects=True, vmem_limit_bytes=56 << 20),
    )(idx, embeddings, codebooks)


def solution(mesh):
    placed = (P("item", None), P(None, "item"), P(None, "center", None))
    return jax.shard_map(
        per_device,
        mesh=mesh,
        in_specs=placed,
        out_specs=(P(None, "center", None), P("item", None)),
        check_vma=False,
    )
```

time: 730 us -> 183 us (0.25)
  waiting for transfers between devices: 586 us -> 0 us
  Pallas kernels: 0 us -> 173 us
  blocking collectives: 56.3 us -> 0 us
  matrix products: 43.8 us -> 0 us
  other arithmetic: 24.9 us -> 0 us
  between operations: 14.2 us -> 0.66 us
    psum x6 -> x0, waiting for transfers between devices: 586 us -> none  [the longest x3 314 us: per_device(): lax.psum(pooled.astype(jnp.bfloat16), 'item').astype(jnp.float32)]
    pallas_call x0 -> x2, Pallas kernels: none -> 173 us  [the longest x1 169 us: per_device(): pl.pallas_call(main_kernel, out_shape=(jax.ShapeDtypeStruct(codebooks.sha...]
    psum x1 -> x0, blocking collectives: 56.3 us -> none  [per_device(): lax.psum(counts.astype(jnp.bfloat16), 'item').astype(jnp.float32)]
    dot_general x6 -> x0, matrix products: 43.8 us -> none  [the longest x3 26.6 us: per_device(): lax.dot_general(onehot, residual, (((0,), (0,)), ((), ())), preferred_ele...]
    convert_element_type x4 -> x0, other arithmetic: 13.5 us -> none  [the longest x3 7.6 us: per_device(): updated = ((summed + prior_weight * previous.astype(jnp.float32)) / (numb...]
  transfers between devices with their start and end apart: 6 -> 0, of which waited for: 6 -> 0; matrix products, arithmetic and copies ran while one was open for 2% -> 0% of each run, Pallas kernels for 0% -> 0%
where the time goes in v1:
time: 183 us
  Pallas kernels  173 us (95%)
  local copies, waits for them, and re-layouts  8.75 us (5%)
    pallas_call x1, Pallas kernels, per_device(): pl.pallas_call(main_kernel, out_shape=(jax.ShapeDtypeStruct(codebooks.sha...  169 us
    unnamed x8, local copies, waits for them, and re-layouts  8.75 us
    pallas_call x1, Pallas kernels, per_device(): pl.pallas_call(prep_kernel, out_shape=jax.ShapeDtypeStruct((ROWS, LANES),...  4.21 us

profile of v1, /device:TPU:0, one launch (start us, length us, event | category | flops | bytes accessed | tf_op | source)
XLA Modules:
  0.0 182.5 jit_solution(7141023055954511312)
XLA Ops:
  0.6 0.0 copy-start.1
  0.6 0.7 copy-done.1
  1.4 4.2 %shard_map.50.idx_ref = s32[80,128]{1,0:T(8,128)S(1)} custom-call(s32[3,2048]{1,0:T(4,128)S(1)} %copy-done.1), custom_call_target="tpu_custom_call" | custom-call | tf_op jit(solution)/shard_map/pallas_call | solution.py:287
  5.6 0.0 copy-start
  5.6 0.6 copy-done
  6.2 168.9 %shard_map.51 = (bf16[3,2048,512]{2,1,0:T(8,128)(2,1)}, bf16[2048,512]{1,0:T(8,128)(2,1)}) custom-call(s32[80,128]{1,0:T(8,128)} %copy-done, bf16[2048,512]{1,0:T(8,128)(2,1)} %emb_ref.1, bf16[3,2048,512]{2,1,0:T(8,128)(2,1)} %cb_ref.1), custom_call_target="tpu_custom_call" | custom-call | tf_op jit(solution)/shard_map/pallas_call | solution.py:295
  175.1 0.0 copy-start.2
  175.1 6.0 %copy.7 = bf16[3,2048,512]{2,1,0:T(8,128)(2,1)} copy(bf16[3,2048,512]{2,1,0:T(8,128)(2,1)} %get-tuple-element.4) | data formatting | bytes 12582912
  181.2 0.0 copy-done.2
  181.2 1.3 copy.8
Async XLA Ops:
  0.6 0.8 copy-start.1
  5.6 0.6 copy-start
  175.1 6.1 %copy-start.2 = (bf16[2048,512]{1,0:T(8,128)(2,1)S(1)}, bf16[2048,512]{1,0:T(8,128)(2,1)}, u32[]{:S(2)}) copy-start(bf16[2048,512]{1,0:T(8,128)(2,1)} %get-tuple-element.5) | copy-start | bytes 6291460

commit v2 on v1

v2 whole, which is shorter than its diff:
```python
import functools

import jax
import jax.numpy as jnp
from jax import lax
from jax.experimental import pallas as pl
from jax.experimental.pallas import tpu as pltpu
from jax.sharding import PartitionSpec as P

MESH = pl.DeviceIdType.MESH
LEVELS, ITEMS, DIM = 3, 2048, 512
N_ITEM, N_CENTER, SHARE, CAP = 16, 8, 128, 32
SLOTS = N_ITEM * CAP
HOP1, HOP2, HOME = 64, 80, ITEMS // N_CENTER
LANES = 128
F32, BF16, I32 = jnp.float32, jnp.bfloat16, jnp.int32


def iota(shape, axis):
    return lax.broadcasted_iota(I32, shape, axis)


def onehot(match):
    return match.astype(F32).astype(BF16)


def dot(a, b):
    return jnp.dot(a, b, preferred_element_type=F32)


ROW_SLOT0 = 0
ROW_OFF = 16
ROW_D1 = 28
ROW_D2 = 40
ROW_D3 = 52
ROW_POS = 64
ROWS = 80


def prep_kernel(codes_ref, out_ref):
    me = lax.axis_index("center")
    a, b = iota((LANES, 2 * LANES), 0), iota((LANES, 2 * LANES), 1)
    before = onehot((b >= LANES) | (a < b))

    def ordered(cls, n_cls, lower=None):
        member = onehot(iota((n_cls, ITEMS), 0) == cls)
        seen = jnp.zeros((n_cls, LANES), F32)
        ranks = []
        for k in range(ITEMS // LANES):
            part = member[:, k * LANES : (k + 1) * LANES]
            both = dot(part, before)
            ranks.append(jnp.sum(part.astype(F32) * (both[:, :LANES] + seen), axis=0, keepdims=True))
            seen = seen + both[:, LANES:]
        rank = jnp.concatenate(ranks, axis=1).astype(I32)
        if lower is None:
            return rank, None
        r, s = iota((n_cls, n_cls), 0), iota((n_cls, n_cls), 1)
        start = jnp.dot(lower(r, s).astype(F32), seen, precision=lax.Precision.HIGHEST, preferred_element_type=F32)
        start = jnp.concatenate([start] * (ITEMS // LANES), axis=1)
        return rank, jnp.sum(member.astype(F32) * start, axis=0, keepdims=True).astype(I32)

    def extract(pos, n_pos, attrs):
        n_hi = n_pos // LANES
        low = onehot(iota((LANES, ITEMS), 0) == jnp.where(pos >= 0, pos % LANES, -1))
        high = iota((8, ITEMS), 0) == jnp.where(pos >= 0, pos // LANES, -1)
        rows = jnp.concatenate([jnp.where(high, at, 0) for at in attrs], axis=0).astype(F32).astype(BF16)
        got = lax.dot_general(rows, low, (((1,), (1,)), ((), ())), preferred_element_type=F32).astype(I32)
        return [got[8 * k : 8 * k + n_hi] for k in range(len(attrs))]

    out_ref[...] = jnp.zeros_like(out_ref)
    shard, off, local = [], [], []
    for lev in range(LEVELS):
        code = codes_ref[lev : lev + 1, :]
        block = code // SHARE
        rank, _ = ordered(block, N_ITEM * N_CENTER)
        slot = (block % N_ITEM) * CAP + rank
        shard.append(code // (SHARE * N_ITEM))
        off.append(code % SHARE)
        local.append(jnp.where(shard[lev] == me, slot, -1))
    for k in range(ITEMS // LANES):
        out_ref[ROW_SLOT0 + k : ROW_SLOT0 + k + 1, :] = local[0][:, k * LANES : (k + 1) * LANES]

    for lev in range(LEVELS):
        here = shard[lev]
        if lev < LEVELS - 1:
            there = shard[lev + 1]
            rank, start = ordered(
                here * N_CENTER + there, N_CENTER * N_CENTER, lambda r, s: (r // N_CENTER == s // N_CENTER) & (s < r)
            )
            order = rank + start
            via, place = order % N_CENTER, order // N_CENTER
            second, _ = ordered(via * N_CENTER + there, N_CENTER * N_CENTER)
            target = [there + 1, second]
            base = HOP2
            pos3 = jnp.where(there == me, via * HOP2 + second, -1)
            slot_next = local[lev + 1]
            hi3, lo3 = extract(pos3, N_CENTER * HOP2, [jnp.maximum(slot_next, 0) // 256 + 1, jnp.maximum(slot_next, 0) % 256])
            d3 = (hi3 - 1) * 256 + lo3
            out_ref[ROW_D3 + 6 * lev : ROW_D3 + 6 * lev + 5, :] = d3
        else:
            rank, start = ordered(here, N_CENTER, lambda r, s: s < r)
            order = rank + start
            via, place = order % N_CENTER, rank // N_CENTER
            target = [jnp.ones_like(order), order // N_CENTER]
            base = HOME
            for k in range(ITEMS // LANES):
                out_ref[ROW_POS + k : ROW_POS + k + 1, :] = (via * HOME + order // N_CENTER)[:, k * LANES : (k + 1) * LANES]
        off_s, via_s, place_s = extract(local[lev], SLOTS, [off[lev] + 1, via + 1, place])
        out_ref[ROW_OFF + 4 * lev : ROW_OFF + 4 * lev + 4, :] = off_s
        out_ref[ROW_D1 + 4 * lev : ROW_D1 + 4 * lev + 4, :] = (via_s - 1) * HOP1 + place_s
        pos2 = jnp.where(via == me, here * HOP1 + place, -1)
        hi2, lo2 = extract(pos2, N_CENTER * HOP1, target)
        out_ref[ROW_D2 + 4 * lev : ROW_D2 + 4 * lev + 4, :] = (hi2 - 1) * base + lo2


CHUNKS = 2
WIDTH = DIM // CHUNKS
ITEM_OFFSETS = [(y, x, c) for y in range(4) for x in range(2) for c in range(2)][1:]
CENTER_OFFSETS = [(h, z) for h in range(2) for z in range(4)][1:]


def main_kernel(
    idx_ref, emb_ref, cb_ref, books_ref, final_ref,
    cb, meta_s, meta_r, dsend, drecv, book, nres, h1s, h1r, h2s, h2r, frecv, scatter, member, assign, sel1, sel2, sel3,
    cb_sem, meta_ss, meta_rs, d_ss, d_rs, g_ss, g_rs, p_rs, h1_ss, h1_rs, h2_ss, h2_rs, f_ss, f_rs, out_sem,
):
    item, center = lax.axis_index("item"), lax.axis_index("center")
    my_y, my_x, my_c = item // 4, (item // 2) % 2, item % 2
    my_h, my_z = center // 4, center % 4

    def item_at(y, x, c):
        return ((my_y + y) % 4) * 4 + ((my_x + x) % 2) * 2 + (my_c + c) % 2

    def center_at(h, z):
        return ((my_h + h) % 2) * 4 + (my_z + z) % 4

    def rows(start, size, step):
        return pl.ds(pl.multiple_of(start * step, step), size)

    barrier = pltpu.get_barrier_semaphore()
    for o in ITEM_OFFSETS:
        pl.semaphore_signal(barrier, inc=1, device_id=(item_at(*o), center), device_id_type=MESH)
    for o in CENTER_OFFSETS:
        pl.semaphore_signal(barrier, inc=1, device_id=(item, center_at(*o)), device_id_type=MESH)

    own_cb = pltpu.make_async_copy(cb_ref.at[:, rows(item, SHARE, SHARE), :], cb, cb_sem)
    own_cb.start()

    def remote(src, dst, ss, rs, to):
        return pltpu.make_async_remote_copy(
            src_ref=src, dst_ref=dst, send_sem=ss, recv_sem=rs, device_id=to, device_id_type=MESH
        )

    def send(src, dst, ss, rs, to):
        cp = remote(src, dst, ss, rs, to)
        cp.start()
        return cp

    def whole(ref, ss, rs):
        return remote(ref, ref, ss, rs, (item, center))

    pending = []

    meta_s[...] = jnp.zeros_like(meta_s)
    for h in range(4):
        for lev in range(LEVELS):
            meta_s[h, lev : lev + 1, :] = idx_ref[ROW_OFF + 4 * lev + h : ROW_OFF + 4 * lev + h + 1, :]

    for k in range(ITEMS // LANES):
        row = idx_ref[ROW_SLOT0 + k : ROW_SLOT0 + k + 1, :]
        scatter[0:SLOTS, k * LANES : (k + 1) * LANES] = onehot(iota((SLOTS, LANES), 0) == row)

    def selection(ref, first, n_in, n_out):
        for k in range(n_in // LANES):
            ref[0:n_out, k * LANES : (k + 1) * LANES] = onehot(
                iota((n_out, LANES), 0) == idx_ref[first + k : first + k + 1, :]
            )

    def select(ref, n_in, n_out, source):
        return dot(ref[0:n_out, 0:n_in], source).astype(BF16)

    def receive_metas():
        whole(meta_r.at[pl.ds(0, 15)], meta_ss, meta_rs).wait_recv()
        own_cb.wait()
        lane = iota((8, LANES), 1)
        mine = (lane >= (item % 4) * CAP) & (lane < (item % 4 + 1) * CAP)
        for q in range(4):
            total = jnp.zeros((8, LANES), I32)
            for j in range(4):
                piece = jnp.where(mine, meta_r[4 * q + j], 0)
                total = total + pltpu.roll(piece, ((j + 4 - item % 4) % 4) * CAP, 1)
            for lev in range(LEVELS):
                member[lev, :, q * LANES : (q + 1) * LANES] = onehot(
                    iota((SHARE, LANES), 0) + 1 == total[lev : lev + 1, :]
                )

    def build_selections(lev):
        selection(sel1.at[lev], ROW_D1 + 4 * lev, SLOTS, N_CENTER * HOP1)
        selection(sel2.at[lev], ROW_D2 + 4 * lev, N_CENTER * HOP1, N_CENTER * HOP2 if lev < LEVELS - 1 else HOME)
        if lev < LEVELS - 1:
            selection(sel3.at[lev], ROW_D3 + 6 * lev, N_CENTER * HOP2, SLOTS)
        for h in range(4):
            row = idx_ref[ROW_OFF + 4 * lev + h : ROW_OFF + 4 * lev + h + 1, :]
            assign[lev, h * LANES : (h + 1) * LANES, :] = (
                (iota((SHARE, LANES), 0) + 1 == row).astype(F32).T.astype(BF16)
            )

    def build_scatter():
        for k in range(ITEMS // LANES):
            row = jnp.broadcast_to(idx_ref[ROW_POS + k : ROW_POS + k + 1, :].astype(F32), (LANES, LANES))
            col = row.T.astype(I32)
            for g in range(ITEMS // LANES):
                scatter[k * LANES : (k + 1) * LANES, g * LANES : (g + 1) * LANES] = onehot(
                    iota((LANES, LANES), 1) + g * LANES == col
                )

    def gather(buf, size, ring, ss, rs, got):
        half = size // 2

        def block(r, p, part=None):
            if part is None:
                return buf.at[rows(ring(r, p)[0], size, size)]
            return buf.at[rows(ring(r, p)[0] * 2 + part, half, half)]

        def move(n, at, to, part=None):
            return send(block(*at, part), block(*at, part), ss, rs.at[n], ring(*to)[1])

        up, down, over = (1, 0), (3, 0), (0, 1)
        own = (0, 0)
        first = [move(0, own, up), move(1, own, down), move(2, own, over)]
        got(*own)
        yield
        first[0].wait_recv()
        a = move(3, down, up, 0)
        first[1].wait_recv()
        d = move(6, up, down, 1)
        got(*down)
        got(*up)
        first[2].wait_recv()
        b = move(4, over, up)
        c = move(5, over, down)
        got(*over)
        yield
        a.wait_recv()
        e = move(7, (2, 0), over, 0)
        d.wait_recv()
        f = move(8, (2, 0), over, 1)
        got(2, 0)
        b.wait_recv()
        got(3, 1)
        c.wait_recv()
        got(1, 1)
        yield
        e.wait_recv()
        f.wait_recv()
        got(2, 1)

    def exchange(src, dst, size, ss, rs):
        own = rows(center, size, size)
        for o in CENTER_OFFSETS:
            to = center_at(*o)
            send(src.at[rows(to, size, size)], dst.at[own], ss, rs, (item, to))
        dst[own, :] = src[own, :]
        cp = whole(dst.at[pl.ds(0, 7 * size)], ss, rs)
        pending.append(cp)
        return cp

    own_rows = rows(item, CAP, CAP)
    own_block = rows(item, SHARE, SHARE)

    def program(k):
        cols = slice(k * WIDTH, (k + 1) * WIDTH)
        last = k == CHUNKS - 1
        dsend[0, k] = dot(scatter[0:SLOTS, :], emb_ref[:, cols]).astype(BF16)
        if k == 0:
            pl.semaphore_wait(barrier, len(ITEM_OFFSETS) + len(CENTER_OFFSETS))
            for o in ITEM_OFFSETS:
                to = item_at(*o)
                send(meta_s.at[to // 4], meta_r.at[item], meta_ss, meta_rs, (to, center))
            meta_r[item] = meta_s[item // 4]
            pending.append(whole(meta_r.at[pl.ds(0, 15)], meta_ss, meta_rs))
        for lev in range(LEVELS):
            mine, theirs, bk = dsend.at[lev, k], drecv.at[lev, k], book.at[lev, k]
            for o in ITEM_OFFSETS:
                to = item_at(*o)
                send(mine.at[rows(to, CAP, CAP)], theirs.at[own_rows], d_ss.at[lev, k], d_rs.at[lev, k], (to, center))
            theirs[own_rows, :] = mine[own_rows, :]
            arrived = whole(theirs.at[pl.ds(0, 15 * CAP)], d_ss.at[lev, k], d_rs.at[lev, k])
            pending.append(arrived)
            if last:
                build_selections(lev)
            yield
            if lev == 0 and k == 0:
                receive_metas()
            arrived.wait_recv()
            count = jnp.sum(member[lev].astype(F32), axis=1, keepdims=True)
            pooled = dot(member[lev], theirs[...])
            bk[own_block, :] = ((pooled + cb[lev, :, cols].astype(F32)) / (count + 1.0)).astype(BF16)
            partner = (item_at(0, 0, 1), center)
            passed = []

            def to_partner(r, p):
                at = bk.at[rows(item_at(r, p, 0), SHARE, SHARE)]
                passed.append(send(at, at, g_ss.at[lev, k], p_rs.at[lev, k, len(passed)], partner))

            yield from gather(
                bk, SHARE, lambda r, p: (item_at(r, p, 0), (item_at(r, p, 0), center)), g_ss.at[lev, k], g_rs.at[lev, k], to_partner
            )
            pending.append(whole(bk.at[pl.ds(0, 15 * SHARE)], g_ss.at[lev, k], g_rs.at[lev, k, 0]))
            yield
            for cp in passed:
                cp.wait_recv()
            pltpu.make_async_copy(bk, books_ref.at[lev, :, cols], out_sem.at[lev, k]).start()
            for b in range(N_ITEM):
                slots = slice(b * CAP, (b + 1) * CAP)
                assigned = dot(assign[lev, slots, :], bk[b * SHARE : (b + 1) * SHARE, :])
                nres[k, slots, :] = (mine[slots, :].astype(F32) - assigned).astype(BF16)
            h1s[lev, k] = select(sel1.at[lev], SLOTS, N_CENTER * HOP1, nres[k])
            hop = exchange(h1s.at[lev, k], h1r.at[lev, k], HOP1, h1_ss.at[lev, k], h1_rs.at[lev, k])
            if last and lev == LEVELS - 1:
                build_scatter()
            yield
            hop.wait_recv()
            if lev < LEVELS - 1:
                h2s[lev, k] = select(sel2.at[lev], N_CENTER * HOP1, N_CENTER * HOP2, h1r[lev, k])
                hop = exchange(h2s.at[lev, k], h2r.at[lev, k], HOP2, h2_ss.at[lev, k], h2_rs.at[lev, k])
                yield
                hop.wait_recv()
                dsend[lev + 1, k] = select(sel3.at[lev], N_CENTER * HOP2, SLOTS, h2r[lev, k])
            else:
                own = rows(center, HOME, HOME)
                frecv[k, own, :] = select(sel2.at[lev], N_CENTER * HOP1, HOME, h1r[lev, k])
                yield from gather(
                    frecv.at[k], HOME, lambda r, p: (center_at(p, r), (item, center_at(p, r))), f_ss.at[k], f_rs.at[k], lambda r, p: None
                )
                pending.append(whole(frecv.at[k, pl.ds(0, 7 * HOME)], f_ss.at[k], f_rs.at[k, 0]))
                for t in range(ITEMS // 256):
                    final_ref[t * 256 : (t + 1) * 256, cols] = dot(
                        scatter[t * 256 : (t + 1) * 256, :], frecv[k]
                    ).astype(BF16)

    running = [program(k) for k in range(CHUNKS)]
    while running:
        running = [p for p in running if next(p, 0) is None]

    for lev in range(LEVELS):
        for k in range(CHUNKS):
            cols = slice(k * WIDTH, (k + 1) * WIDTH)
            pltpu.make_async_copy(book.at[lev, k], books_ref.at[lev, :, cols], out_sem.at[lev, k]).wait()
    for cp in pending:
        cp.wait_send()


PART = 512
PARTS = (LEVELS + 1) * (ITEMS // PART)


def copy_kernel(a_ref, b_ref, oa_ref, ob_ref, hold, in_sem, out_sem):
    pairs = []
    for t in range(ITEMS // PART):
        part = pl.ds(t * PART, PART)
        pairs += [(a_ref.at[lev, part], oa_ref.at[lev, part]) for lev in range(LEVELS)] + [(b_ref.at[part], ob_ref.at[part])]
    ins = [pltpu.make_async_copy(src, hold.at[n], in_sem.at[n]) for n, (src, _) in enumerate(pairs)]
    outs = [pltpu.make_async_copy(hold.at[n], dst, out_sem.at[n]) for n, (_, dst) in enumerate(pairs)]
    for cp in ins:
        cp.start()
    for i, o in zip(ins, outs):
        i.wait()
        o.start()
    for cp in outs:
        cp.wait()


def per_device(embeddings, codes, codebooks):
    vmem = pl.BlockSpec(memory_space=pltpu.VMEM)
    hbm = pl.BlockSpec(memory_space=pl.ANY)
    idx = pl.pallas_call(
        prep_kernel,
        out_shape=jax.ShapeDtypeStruct((ROWS, LANES), I32),
        in_specs=[vmem],
        out_specs=vmem,
        compiler_params=pltpu.CompilerParams(vmem_limit_bytes=48 << 20),
    )(codes)
    dma = pltpu.SemaphoreType.DMA
    outs = (
        jax.ShapeDtypeStruct(codebooks.shape, BF16),
        jax.ShapeDtypeStruct(embeddings.shape, BF16),
    )
    by_chunk = (LEVELS, CHUNKS)
    books, final = pl.pallas_call(
        main_kernel,
        out_shape=outs,
        in_specs=[vmem, vmem, hbm],
        out_specs=(hbm, vmem),
        scratch_shapes=[
            pltpu.VMEM((LEVELS, SHARE, DIM), BF16),
            pltpu.VMEM((4, 8, LANES), I32),
            pltpu.VMEM((N_ITEM, 8, LANES), I32),
            pltpu.VMEM((*by_chunk, SLOTS, WIDTH), BF16),
            pltpu.VMEM((*by_chunk, SLOTS, WIDTH), BF16),
            pltpu.VMEM((*by_chunk, N_ITEM * SHARE, WIDTH), BF16),
            pltpu.VMEM((CHUNKS, SLOTS, WIDTH), BF16),
            pltpu.VMEM((*by_chunk, N_CENTER * HOP1, WIDTH), BF16),
            pltpu.VMEM((*by_chunk, N_CENTER * HOP1, WIDTH), BF16),
            pltpu.VMEM((LEVELS - 1, CHUNKS, N_CENTER * HOP2, WIDTH), BF16),
            pltpu.VMEM((LEVELS - 1, CHUNKS, N_CENTER * HOP2, WIDTH), BF16),
            pltpu.VMEM((CHUNKS, ITEMS, WIDTH), BF16),
            pltpu.VMEM((ITEMS, ITEMS), BF16),
            pltpu.VMEM((LEVELS, SHARE, SLOTS), BF16),
            pltpu.VMEM((LEVELS, SLOTS, SHARE), BF16),
            pltpu.VMEM((LEVELS, N_CENTER * HOP1, SLOTS), BF16),
            pltpu.VMEM((LEVELS, N_CENTER * HOP2, N_CENTER * HOP1), BF16),
            pltpu.VMEM((LEVELS - 1, SLOTS, N_CENTER * HOP2), BF16),
            dma,
            dma, dma,
            dma(by_chunk), dma(by_chunk),
            dma(by_chunk), dma((*by_chunk, 9)), dma((*by_chunk, 8)),
            dma(by_chunk), dma(by_chunk),
            dma(by_chunk), dma(by_chunk),
            dma((CHUNKS,)), dma((CHUNKS, 9)),
            dma(by_chunk),
        ],
        compiler_params=pltpu.CompilerParams(collective_id=0, has_side_effects=True, vmem_limit_bytes=60 << 20),
    )(idx, embeddings, codebooks)
    return pl.pallas_call(
        copy_kernel,
        out_shape=outs,
        in_specs=[hbm, hbm],
        out_specs=(hbm, hbm),
        scratch_shapes=[pltpu.VMEM((PARTS, PART, DIM), BF16), dma((PARTS,)), dma((PARTS,))],
        compiler_params=pltpu.CompilerParams(vmem_limit_bytes=60 << 20),
    )(books, final)


def solution(mesh):
    placed = (P("item", None), P(None, "item"), P(None, "center", None))
    return jax.shard_map(
        per_device,
        mesh=mesh,
        in_specs=placed,
        out_specs=(P(None, "center", None), P("item", None)),
        check_vma=False,
    )
```

time: 183 us -> 144 us (0.79)
  Pallas kernels: 173 us -> 141 us
  local copies, waits for them, and re-layouts: 8.75 us -> 1.39 us
    pallas_call x1 -> x2, Pallas kernels: 169 us -> 137 us  [the longest x1 130 us: per_device(): pl.pallas_call(main_kernel, out_shape=outs, in_specs=[vmem, vmem, hbm], o...]
    unnamed x8 -> x4, local copies, waits for them, and re-layouts: 8.75 us -> 1.39 us
where the time goes in v2:
time: 144 us; the launch traced here: 143 us
  Pallas kernels  141 us (98%)
    pallas_call x1, Pallas kernels, per_device(): pl.pallas_call(main_kernel, out_shape=outs, in_specs=[vmem, vmem, hbm], o...  130 us
    pallas_call x1, Pallas kernels, per_device(): pl.pallas_call(copy_kernel, out_shape=outs, in_specs=[hbm, hbm], out_spec...  6.57 us
    pallas_call x1, Pallas kernels, per_device(): pl.pallas_call(prep_kernel, out_shape=jax.ShapeDtypeStruct((ROWS, LANES),...  4.21 us

profile of v2, /device:TPU:0, one launch (start us, length us, event | category | flops | bytes accessed | tf_op | source)
XLA Modules:
  0.0 143.4 jit_solution(10498134162277300306)
XLA Ops:
  0.6 0.0 copy-start.1
  0.6 0.7 copy-done.1
  1.4 4.2 %shard_map.50.idx_ref = s32[80,128]{1,0:T(8,128)S(1)} custom-call(s32[3,2048]{1,0:T(4,128)S(1)} %copy-done.1), custom_call_target="tpu_custom_call" | custom-call | tf_op jit(solution)/shard_map/pallas_call | solution.py:377
  5.6 0.0 copy-start
  5.6 0.6 copy-done
  6.2 130.4 %shard_map.51 = (bf16[3,2048,512]{2,1,0:T(8,128)(2,1)}, bf16[2048,512]{1,0:T(8,128)(2,1)}) custom-call(s32[80,128]{1,0:T(8,128)} %copy-done, bf16[2048,512]{1,0:T(8,128)(2,1)} %emb_ref.1, bf16[3,2048,512]{2,1,0:T(8,128)(2,1)} %cb_ref.1), custom_call_target="tpu_custom_call" | custom-call | tf_op jit(solution)/shard_map/pallas_call | solution.py:390
  136.7 6.6 %shard_map.52 = (bf16[3,2048,512]{2,1,0:T(8,128)(2,1)}, bf16[2048,512]{1,0:T(8,128)(2,1)}) custom-call(bf16[3,2048,512]{2,1,0:T(8,128)(2,1)} %get-tuple-element.4.a_ref, bf16[2048,512]{1,0:T(8,128)(2,1)} %get-tuple-element.5.b_ref), custom_call_target="tpu_custom_call" | custom-call | tf_op jit(solution)/shard_map/pallas_call | solution.py:425
Async XLA Ops:
  0.6 0.8 copy-start.1
  5.6 0.6 copy-start

commit v3 on v2

--- a/solution.py
+++ b/solution.py
@@ -121,8 +121,9 @@
 
 def main_kernel(
     idx_ref, emb_ref, cb_ref, books_ref, final_ref,
-    cb, meta_s, meta_r, dsend, drecv, book, nres, h1s, h1r, h2s, h2r, frecv, scatter, member, assign, sel1, sel2, sel3,
-    cb_sem, meta_ss, meta_rs, d_ss, d_rs, g_ss, g_rs, p_rs, h1_ss, h1_rs, h2_ss, h2_rs, f_ss, f_rs, out_sem,
+    cb, meta_s, meta_r, dsend, drecv, rsend, rrecv, book, h1s, h1r, h2s, h2r, frecv, scatter, member, members, total,
+    sel1, sel2, sel3,
+    cb_sem, meta_ss, meta_rs, d_ss, d_rs, r_ss, r_rs, g_ss, g_rs, p_rs, h1_ss, h1_rs, h2_ss, h2_rs, f_ss, f_rs, out_sem,
 ):
     item, center = lax.axis_index("item"), lax.axis_index("center")
     my_y, my_x, my_c = item // 4, (item // 2) % 2, item % 2
@@ -185,25 +186,23 @@
         lane = iota((8, LANES), 1)
         mine = (lane >= (item % 4) * CAP) & (lane < (item % 4 + 1) * CAP)
         for q in range(4):
-            total = jnp.zeros((8, LANES), I32)
+            codes = jnp.zeros((8, LANES), I32)
             for j in range(4):
                 piece = jnp.where(mine, meta_r[4 * q + j], 0)
-                total = total + pltpu.roll(piece, ((j + 4 - item % 4) % 4) * CAP, 1)
+                codes = codes + pltpu.roll(piece, ((j + 4 - item % 4) % 4) * CAP, 1)
             for lev in range(LEVELS):
-                member[lev, :, q * LANES : (q + 1) * LANES] = onehot(
-                    iota((SHARE, LANES), 0) + 1 == total[lev : lev + 1, :]
-                )
+                part = (iota((SHARE, LANES), 0) + 1 == codes[lev : lev + 1, :]).astype(F32)
+                member[lev, :, q * LANES : (q + 1) * LANES] = part.astype(BF16)
+                members[lev, q * LANES : (q + 1) * LANES, :] = part.T.astype(BF16)
+        for lev in range(LEVELS):
+            count = jnp.sum(member[lev].astype(F32), axis=1, keepdims=True)
+            total[lev] = jnp.broadcast_to(count + 1.0, (SHARE, LANES))
 
     def build_selections(lev):
         selection(sel1.at[lev], ROW_D1 + 4 * lev, SLOTS, N_CENTER * HOP1)
         selection(sel2.at[lev], ROW_D2 + 4 * lev, N_CENTER * HOP1, N_CENTER * HOP2 if lev < LEVELS - 1 else HOME)
         if lev < LEVELS - 1:
             selection(sel3.at[lev], ROW_D3 + 6 * lev, N_CENTER * HOP2, SLOTS)
-        for h in range(4):
-            row = idx_ref[ROW_OFF + 4 * lev + h : ROW_OFF + 4 * lev + h + 1, :]
-            assign[lev, h * LANES : (h + 1) * LANES, :] = (
-                (iota((SHARE, LANES), 0) + 1 == row).astype(F32).T.astype(BF16)
-            )
 
     def build_scatter():
         for k in range(ITEMS // LANES):
@@ -214,46 +213,68 @@
                     iota((LANES, LANES), 1) + g * LANES == col
                 )
 
-    def gather(buf, size, ring, ss, rs, got):
-        half = size // 2
-
-        def block(r, p, part=None):
+    def mover(buf, size, ring, ss, rs):
+        def move(n, at, to, part=None):
+            index = ring(*at)[0]
             if part is None:
-                return buf.at[rows(ring(r, p)[0], size, size)]
-            return buf.at[rows(ring(r, p)[0] * 2 + part, half, half)]
-
-        def move(n, at, to, part=None):
-            return send(block(*at, part), block(*at, part), ss, rs.at[n], ring(*to)[1])
-
-        up, down, over = (1, 0), (3, 0), (0, 1)
-        own = (0, 0)
+                piece = buf.at[rows(index, size, size)]
+            else:
+                piece = buf.at[rows(index * 2 + part, size // 2, size // 2)]
+            return send(piece, piece, ss, rs.at[n], ring(*to)[1])
+
+        return move
+
+    own, up, down, over = (0, 0), (1, 0), (3, 0), (0, 1)
+
+    def gather_rows(k):
+        move = mover(frecv.at[k], HOME, lambda z, h: (center_at(h, z), (item, center_at(h, z))), f_ss.at[k], f_rs.at[k])
         first = [move(0, own, up), move(1, own, down), move(2, own, over)]
-        got(*own)
         yield
         first[0].wait_recv()
         a = move(3, down, up, 0)
         first[1].wait_recv()
-        d = move(6, up, down, 1)
-        got(*down)
-        got(*up)
+        d = move(4, up, down, 1)
         first[2].wait_recv()
-        b = move(4, over, up)
-        c = move(5, over, down)
-        got(*over)
+        rest = [move(5, over, up), move(6, over, down)]
         yield
         a.wait_recv()
-        e = move(7, (2, 0), over, 0)
+        rest.append(move(7, (2, 0), over, 0))
         d.wait_recv()
-        f = move(8, (2, 0), over, 1)
-        got(2, 0)
-        b.wait_recv()
-        got(3, 1)
-        c.wait_recv()
-        got(1, 1)
-        yield
-        e.wait_recv()
-        f.wait_recv()
-        got(2, 1)
+        rest.append(move(8, (2, 0), over, 1))
+        yield
+        for cp in rest:
+            cp.wait_recv()
+
+    def gather_books(lev, k):
+        bk, cols = book.at[lev, k], slice(k * WIDTH, (k + 1) * WIDTH)
+        move = mover(
+            bk, SHARE,
+            lambda y, x: (my_c * 8 + item_at(y, x, 0) // 2, (item_at(y, x, 0), center)),
+            g_ss.at[lev, k], g_rs.at[lev, k],
+        )
+        first = [move(0, own, up), move(1, own, down), move(2, own, over)]
+        yield
+        for cp in first:
+            cp.wait_recv()
+        second = [move(3, down, up, 0), move(4, up, down, 1), move(5, over, up), move(6, over, down)]
+        yield
+        second[2].wait_recv()
+        third = [move(7, (3, 1), up, 0)]
+        second[3].wait_recv()
+        third.append(move(8, (1, 1), down, 1))
+        yield
+        for cp in second[:2] + third:
+            cp.wait_recv()
+        half = bk.at[rows(my_c, 8 * SHARE, 8 * SHARE)]
+        passed = send(half, half, g_ss.at[lev, k], p_rs.at[lev, k], (item_at(0, 0, 1), center))
+        yield
+        passed.wait_recv()
+        for c in range(2):
+            for q in range(8):
+                pltpu.make_async_copy(
+                    bk.at[pl.ds((c * 8 + q) * SHARE, SHARE)], books_ref.at[lev, q, c, :, cols], out_sem.at[lev, k]
+                ).start()
+        pending.append(whole(bk.at[pl.ds(0, 15 * SHARE)], g_ss.at[lev, k], p_rs.at[lev, k]))
 
     def exchange(src, dst, size, ss, rs):
         own = rows(center, size, size)
@@ -265,12 +286,24 @@
         pending.append(cp)
         return cp
 
-    own_rows = rows(item, CAP, CAP)
-    own_block = rows(item, SHARE, SHARE)
+    def swap(src, dst, ss, rs):
+        own_rows = rows(item, CAP, CAP)
+        for o in ITEM_OFFSETS:
+            to = item_at(*o)
+            send(src.at[rows(to, CAP, CAP)], dst.at[own_rows], ss, rs, (to, center))
+        dst[own_rows, :] = src[own_rows, :]
+        cp = whole(dst.at[pl.ds(0, 15 * CAP)], ss, rs)
+        pending.append(cp)
+        return cp
 
     def program(k):
         cols = slice(k * WIDTH, (k + 1) * WIDTH)
         last = k == CHUNKS - 1
+        background = []
+
+        def step():
+            background[:] = [g for g in background if next(g, 0) is None]
+
         dsend[0, k] = dot(scatter[0:SLOTS, :], emb_ref[:, cols]).astype(BF16)
         if k == 0:
             pl.semaphore_wait(barrier, len(ITEM_OFFSETS) + len(CENTER_OFFSETS))
@@ -280,43 +313,28 @@
             meta_r[item] = meta_s[item // 4]
             pending.append(whole(meta_r.at[pl.ds(0, 15)], meta_ss, meta_rs))
         for lev in range(LEVELS):
-            mine, theirs, bk = dsend.at[lev, k], drecv.at[lev, k], book.at[lev, k]
-            for o in ITEM_OFFSETS:
-                to = item_at(*o)
-                send(mine.at[rows(to, CAP, CAP)], theirs.at[own_rows], d_ss.at[lev, k], d_rs.at[lev, k], (to, center))
-            theirs[own_rows, :] = mine[own_rows, :]
-            arrived = whole(theirs.at[pl.ds(0, 15 * CAP)], d_ss.at[lev, k], d_rs.at[lev, k])
-            pending.append(arrived)
+            arrived = swap(dsend.at[lev, k], drecv.at[lev, k], d_ss.at[lev, k], d_rs.at[lev, k])
+            step()
             if last:
                 build_selections(lev)
             yield
             if lev == 0 and k == 0:
                 receive_metas()
             arrived.wait_recv()
-            count = jnp.sum(member[lev].astype(F32), axis=1, keepdims=True)
-            pooled = dot(member[lev], theirs[...])
-            bk[own_block, :] = ((pooled + cb[lev, :, cols].astype(F32)) / (count + 1.0)).astype(BF16)
-            partner = (item_at(0, 0, 1), center)
-            passed = []
-
-            def to_partner(r, p):
-                at = bk.at[rows(item_at(r, p, 0), SHARE, SHARE)]
-                passed.append(send(at, at, g_ss.at[lev, k], p_rs.at[lev, k, len(passed)], partner))
-
-            yield from gather(
-                bk, SHARE, lambda r, p: (item_at(r, p, 0), (item_at(r, p, 0), center)), g_ss.at[lev, k], g_rs.at[lev, k], to_partner
-            )
-            pending.append(whole(bk.at[pl.ds(0, 15 * SHARE)], g_ss.at[lev, k], g_rs.at[lev, k, 0]))
+            pooled = dot(member[lev], drecv[lev, k])
+            size = jnp.concatenate([total[lev]] * (WIDTH // LANES), axis=1)
+            updated = ((pooled + cb[lev, :, cols].astype(F32)) / size).astype(BF16)
+            rsend[lev, k] = (drecv[lev, k].astype(F32) - dot(members[lev], updated)).astype(BF16)
+            arrived = swap(rsend.at[lev, k], rrecv.at[lev, k], r_ss.at[lev, k], r_rs.at[lev, k])
+            book[lev, k, rows(my_c * 8 + item // 2, SHARE, SHARE), :] = updated
+            step()
+            background.append(gather_books(lev, k))
+            next(background[-1])
             yield
-            for cp in passed:
-                cp.wait_recv()
-            pltpu.make_async_copy(bk, books_ref.at[lev, :, cols], out_sem.at[lev, k]).start()
-            for b in range(N_ITEM):
-                slots = slice(b * CAP, (b + 1) * CAP)
-                assigned = dot(assign[lev, slots, :], bk[b * SHARE : (b + 1) * SHARE, :])
-                nres[k, slots, :] = (mine[slots, :].astype(F32) - assigned).astype(BF16)
-            h1s[lev, k] = select(sel1.at[lev], SLOTS, N_CENTER * HOP1, nres[k])
+            arrived.wait_recv()
+            h1s[lev, k] = select(sel1.at[lev], SLOTS, N_CENTER * HOP1, rrecv[lev, k])
             hop = exchange(h1s.at[lev, k], h1r.at[lev, k], HOP1, h1_ss.at[lev, k], h1_rs.at[lev, k])
+            step()
             if last and lev == LEVELS - 1:
                 build_scatter()
             yield
@@ -324,15 +342,17 @@
             if lev < LEVELS - 1:
                 h2s[lev, k] = select(sel2.at[lev], N_CENTER * HOP1, N_CENTER * HOP2, h1r[lev, k])
                 hop = exchange(h2s.at[lev, k], h2r.at[lev, k], HOP2, h2_ss.at[lev, k], h2_rs.at[lev, k])
+                step()
                 yield
                 hop.wait_recv()
                 dsend[lev + 1, k] = select(sel3.at[lev], N_CENTER * HOP2, SLOTS, h2r[lev, k])
             else:
-                own = rows(center, HOME, HOME)
-                frecv[k, own, :] = select(sel2.at[lev], N_CENTER * HOP1, HOME, h1r[lev, k])
-                yield from gather(
-                    frecv.at[k], HOME, lambda r, p: (center_at(p, r), (item, center_at(p, r))), f_ss.at[k], f_rs.at[k], lambda r, p: None
-                )
+                frecv[k, rows(center, HOME, HOME), :] = select(sel2.at[lev], N_CENTER * HOP1, HOME, h1r[lev, k])
+                for _ in gather_rows(k):
+                    step()
+                    yield
+                while background:
+                    step()
                 pending.append(whole(frecv.at[k, pl.ds(0, 7 * HOME)], f_ss.at[k], f_rs.at[k, 0]))
                 for t in range(ITEMS // 256):
                     final_ref[t * 256 : (t + 1) * 256, cols] = dot(
@@ -345,8 +365,7 @@
 
     for lev in range(LEVELS):
         for k in range(CHUNKS):
-            cols = slice(k * WIDTH, (k + 1) * WIDTH)
-            pltpu.make_async_copy(book.at[lev, k], books_ref.at[lev, :, cols], out_sem.at[lev, k]).wait()
+            pltpu.make_async_copy(book.at[lev, k], book.at[lev, k], out_sem.at[lev, k]).wait()
     for cp in pending:
         cp.wait_send()
 
@@ -389,7 +408,7 @@
     by_chunk = (LEVELS, CHUNKS)
     books, final = pl.pallas_call(
         main_kernel,
-        out_shape=outs,
+        out_shape=(jax.ShapeDtypeStruct((LEVELS, N_ITEM // 2, 2, SHARE, DIM), BF16), outs[1]),
         in_specs=[vmem, vmem, hbm],
         out_specs=(hbm, vmem),
         scratch_shapes=[
@@ -398,8 +417,9 @@
             pltpu.VMEM((N_ITEM, 8, LANES), I32),
             pltpu.VMEM((*by_chunk, SLOTS, WIDTH), BF16),
             pltpu.VMEM((*by_chunk, SLOTS, WIDTH), BF16),
+            pltpu.VMEM((*by_chunk, SLOTS, WIDTH), BF16),
+            pltpu.VMEM((*by_chunk, SLOTS, WIDTH), BF16),
             pltpu.VMEM((*by_chunk, N_ITEM * SHARE, WIDTH), BF16),
-            pltpu.VMEM((CHUNKS, SLOTS, WIDTH), BF16),
             pltpu.VMEM((*by_chunk, N_CENTER * HOP1, WIDTH), BF16),
             pltpu.VMEM((*by_chunk, N_CENTER * HOP1, WIDTH), BF16),
             pltpu.VMEM((LEVELS - 1, CHUNKS, N_CENTER * HOP2, WIDTH), BF16),
@@ -408,13 +428,15 @@
             pltpu.VMEM((ITEMS, ITEMS), BF16),
             pltpu.VMEM((LEVELS, SHARE, SLOTS), BF16),
             pltpu.VMEM((LEVELS, SLOTS, SHARE), BF16),
+            pltpu.VMEM((LEVELS, SHARE, LANES), F32),
             pltpu.VMEM((LEVELS, N_CENTER * HOP1, SLOTS), BF16),
             pltpu.VMEM((LEVELS, N_CENTER * HOP2, N_CENTER * HOP1), BF16),
             pltpu.VMEM((LEVELS - 1, SLOTS, N_CENTER * HOP2), BF16),
             dma,
             dma, dma,
             dma(by_chunk), dma(by_chunk),
-            dma(by_chunk), dma((*by_chunk, 9)), dma((*by_chunk, 8)),
+            dma(by_chunk), dma(by_chunk),
+            dma(by_chunk), dma((*by_chunk, 9)), dma(by_chunk),
             dma(by_chunk), dma(by_chunk),
             dma(by_chunk), dma(by_chunk),
             dma((CHUNKS,)), dma((CHUNKS, 9)),
@@ -429,7 +451,7 @@
         out_specs=(hbm, hbm),
         scratch_shapes=[pltpu.VMEM((PARTS, PART, DIM), BF16), dma((PARTS,)), dma((PARTS,))],
         compiler_params=pltpu.CompilerParams(vmem_limit_bytes=60 << 20),
-    )(books, final)
+    )(books.reshape(codebooks.shape), final)
 
 
 def solution(mesh):

time: 144 us -> 127 us (0.88)
  Pallas kernels: 141 us -> 125 us
    pallas_call x1, Pallas kernels: 130 us -> 114 us  [per_device(): pl.pallas_call(main_kernel, out_shape=(jax.ShapeDtypeStruct((LEVELS, N_IT...]
where the time goes in v3:
time: 127 us
  Pallas kernels  125 us (98%)
  local copies, waits for them, and re-layouts  1.39 us (1%)
    pallas_call x1, Pallas kernels, per_device(): pl.pallas_call(main_kernel, out_shape=(jax.ShapeDtypeStruct((LEVELS, N_IT...  114 us
    pallas_call x1, Pallas kernels, per_device(): pl.pallas_call(copy_kernel, out_shape=outs, in_specs=[hbm, hbm], out_spec...  6.57 us
    pallas_call x1, Pallas kernels, per_device(): pl.pallas_call(prep_kernel, out_shape=jax.ShapeDtypeStruct((ROWS, LANES),...  4.21 us

profile of v3, /device:TPU:0, one launch (start us, length us, event | category | flops | bytes accessed | tf_op | source)
XLA Modules:
  0.0 127.2 jit_solution(2871430772208660571)
XLA Ops:
  0.6 0.0 copy-start.1
  0.6 0.7 copy-done.1
  1.4 4.2 %shard_map.50.idx_ref = s32[80,128]{1,0:T(8,128)S(1)} custom-call(s32[3,2048]{1,0:T(4,128)S(1)} %copy-done.1), custom_call_target="tpu_custom_call" | custom-call | tf_op jit(solution)/shard_map/pallas_call | solution.py:396
  5.6 0.0 copy-start
  5.6 0.6 copy-done
  6.2 114.3 %shard_map.51 = (bf16[3,8,2,128,512]{4,3,2,1,0:T(8,128)(2,1)}, bf16[2048,512]{1,0:T(8,128)(2,1)}) custom-call(s32[80,128]{1,0:T(8,128)} %copy-done, bf16[2048,512]{1,0:T(8,128)(2,1)} %emb_ref.1, bf16[3,2048,512]{2,1,0:T(8,128)(2,1)} %cb_ref.1), custom_call_target="tpu_custom_call" | custom-call | tf_op jit(solution)/shard_map/pallas_call | solution.py:409
  120.5 6.6 %shard_map.52 = (bf16[3,2048,512]{2,1,0:T(8,128)(2,1)}, bf16[2048,512]{1,0:T(8,128)(2,1)}) custom-call(bf16[3,2048,512]{2,1,0:T(8,128)(2,1)} %bitcast.1, bf16[2048,512]{1,0:T(8,128)(2,1)} %get-tuple-element.5.b_ref), custom_call_target="tpu_custom_call" | custom-call | tf_op jit(solution)/shard_map/pallas_call | solution.py:447
Async XLA Ops:
  0.6 0.8 copy-start.1
  5.6 0.6 copy-start

commit v4 on v3

--- a/solution.py
+++ b/solution.py
@@ -28,89 +28,80 @@
     return jnp.dot(a, b, preferred_element_type=F32)
 
 
-ROW_SLOT0 = 0
-ROW_OFF = 16
-ROW_D1 = 28
-ROW_D2 = 40
-ROW_D3 = 52
-ROW_POS = 64
-ROWS = 80
-
-
-def prep_kernel(codes_ref, out_ref):
-    me = lax.axis_index("center")
+ROW_OFF = 0
+ROW_D1 = 12
+ROW_D2 = 24
+ROW_D3 = 36
+ROW_POS = 48
+ROWS = 64
+
+
+def ordered(cls, n_cls, lower=None):
     a, b = iota((LANES, 2 * LANES), 0), iota((LANES, 2 * LANES), 1)
     before = onehot((b >= LANES) | (a < b))
-
-    def ordered(cls, n_cls, lower=None):
-        member = onehot(iota((n_cls, ITEMS), 0) == cls)
-        seen = jnp.zeros((n_cls, LANES), F32)
-        ranks = []
+    member = onehot(iota((n_cls, ITEMS), 0) == cls)
+    seen = jnp.zeros((n_cls, LANES), F32)
+    ranks = []
+    for k in range(ITEMS // LANES):
+        part = member[:, k * LANES : (k + 1) * LANES]
+        both = dot(part, before)
+        ranks.append(jnp.sum(part.astype(F32) * (both[:, :LANES] + seen), axis=0, keepdims=True))
+        seen = seen + both[:, LANES:]
+    rank = jnp.concatenate(ranks, axis=1).astype(I32)
+    if lower is None:
+        return rank, None
+    r, s = iota((n_cls, n_cls), 0), iota((n_cls, n_cls), 1)
+    start = jnp.dot(lower(r, s).astype(F32), seen, precision=lax.Precision.HIGHEST, preferred_element_type=F32)
+    start = jnp.concatenate([start] * (ITEMS // LANES), axis=1)
+    return rank, jnp.sum(member.astype(F32) * start, axis=0, keepdims=True).astype(I32)
+
+
+def extract(pos, n_pos, attrs):
+    n_hi = n_pos // LANES
+    low = onehot(iota((LANES, ITEMS), 0) == jnp.where(pos >= 0, pos & (LANES - 1), -1))
+    high = iota((8, ITEMS), 0) == jnp.where(pos >= 0, pos >> 7, -1)
+    rows = jnp.concatenate([jnp.where(high, at, 0) for at in attrs], axis=0).astype(F32).astype(BF16)
+    got = lax.dot_general(rows, low, (((1,), (1,)), ((), ())), preferred_element_type=F32).astype(I32)
+    return [got[8 * k : 8 * k + n_hi] for k in range(len(attrs))]
+
+
+def slots_of(codes_ref, lev, me):
+    code = codes_ref[lev : lev + 1, :]
+    block = code >> 7
+    rank, _ = ordered(block, N_ITEM * N_CENTER)
+    shard = code >> 11
+    return shard, code & (SHARE - 1), jnp.where(shard == me, (block & (N_ITEM - 1)) * CAP + rank, -1)
+
+
+def prepare_codes(idx, lev, off, local):
+    idx[ROW_OFF + 4 * lev : ROW_OFF + 4 * lev + 4, :] = extract(local, SLOTS, [off + 1])[0]
+
+
+def prepare_moves(idx, lev, me, here, local, there, slot_next):
+    if lev < LEVELS - 1:
+        rank, start = ordered(here * N_CENTER + there, N_CENTER * N_CENTER, lambda r, s: (r // N_CENTER == s // N_CENTER) & (s < r))
+        order = rank + start
+        via, place = order & 7, order >> 3
+        second, _ = ordered(via * N_CENTER + there, N_CENTER * N_CENTER)
+        target = [there + 1, second]
+        base = HOP2
+        pos3 = jnp.where(there == me, via * HOP2 + second, -1)
+        slot_next = jnp.maximum(slot_next, 0)
+        hi3, lo3 = extract(pos3, N_CENTER * HOP2, [(slot_next >> 8) + 1, slot_next & 255])
+        idx[ROW_D3 + 6 * lev : ROW_D3 + 6 * lev + 5, :] = (hi3 - 1) * 256 + lo3
+    else:
+        rank, start = ordered(here, N_CENTER, lambda r, s: s < r)
+        order = rank + start
+        via, place = order & 7, rank >> 3
+        target = [jnp.ones_like(order), order >> 3]
+        base = HOME
         for k in range(ITEMS // LANES):
-            part = member[:, k * LANES : (k + 1) * LANES]
-            both = dot(part, before)
-            ranks.append(jnp.sum(part.astype(F32) * (both[:, :LANES] + seen), axis=0, keepdims=True))
-            seen = seen + both[:, LANES:]
-        rank = jnp.concatenate(ranks, axis=1).astype(I32)
-        if lower is None:
-            return rank, None
-        r, s = iota((n_cls, n_cls), 0), iota((n_cls, n_cls), 1)
-        start = jnp.dot(lower(r, s).astype(F32), seen, precision=lax.Precision.HIGHEST, preferred_element_type=F32)
-        start = jnp.concatenate([start] * (ITEMS // LANES), axis=1)
-        return rank, jnp.sum(member.astype(F32) * start, axis=0, keepdims=True).astype(I32)
-
-    def extract(pos, n_pos, attrs):
-        n_hi = n_pos // LANES
-        low = onehot(iota((LANES, ITEMS), 0) == jnp.where(pos >= 0, pos % LANES, -1))
-        high = iota((8, ITEMS), 0) == jnp.where(pos >= 0, pos // LANES, -1)
-        rows = jnp.concatenate([jnp.where(high, at, 0) for at in attrs], axis=0).astype(F32).astype(BF16)
-        got = lax.dot_general(rows, low, (((1,), (1,)), ((), ())), preferred_element_type=F32).astype(I32)
-        return [got[8 * k : 8 * k + n_hi] for k in range(len(attrs))]
-
-    out_ref[...] = jnp.zeros_like(out_ref)
-    shard, off, local = [], [], []
-    for lev in range(LEVELS):
-        code = codes_ref[lev : lev + 1, :]
-        block = code // SHARE
-        rank, _ = ordered(block, N_ITEM * N_CENTER)
-        slot = (block % N_ITEM) * CAP + rank
-        shard.append(code // (SHARE * N_ITEM))
-        off.append(code % SHARE)
-        local.append(jnp.where(shard[lev] == me, slot, -1))
-    for k in range(ITEMS // LANES):
-        out_ref[ROW_SLOT0 + k : ROW_SLOT0 + k + 1, :] = local[0][:, k * LANES : (k + 1) * LANES]
-
-    for lev in range(LEVELS):
-        here = shard[lev]
-        if lev < LEVELS - 1:
-            there = shard[lev + 1]
-            rank, start = ordered(
-                here * N_CENTER + there, N_CENTER * N_CENTER, lambda r, s: (r // N_CENTER == s // N_CENTER) & (s < r)
-            )
-            order = rank + start
-            via, place = order % N_CENTER, order // N_CENTER
-            second, _ = ordered(via * N_CENTER + there, N_CENTER * N_CENTER)
-            target = [there + 1, second]
-            base = HOP2
-            pos3 = jnp.where(there == me, via * HOP2 + second, -1)
-            slot_next = local[lev + 1]
-            hi3, lo3 = extract(pos3, N_CENTER * HOP2, [jnp.maximum(slot_next, 0) // 256 + 1, jnp.maximum(slot_next, 0) % 256])
-            d3 = (hi3 - 1) * 256 + lo3
-            out_ref[ROW_D3 + 6 * lev : ROW_D3 + 6 * lev + 5, :] = d3
-        else:
-            rank, start = ordered(here, N_CENTER, lambda r, s: s < r)
-            order = rank + start
-            via, place = order % N_CENTER, rank // N_CENTER
-            target = [jnp.ones_like(order), order // N_CENTER]
-            base = HOME
-            for k in range(ITEMS // LANES):
-                out_ref[ROW_POS + k : ROW_POS + k + 1, :] = (via * HOME + order // N_CENTER)[:, k * LANES : (k + 1) * LANES]
-        off_s, via_s, place_s = extract(local[lev], SLOTS, [off[lev] + 1, via + 1, place])
-        out_ref[ROW_OFF + 4 * lev : ROW_OFF + 4 * lev + 4, :] = off_s
-        out_ref[ROW_D1 + 4 * lev : ROW_D1 + 4 * lev + 4, :] = (via_s - 1) * HOP1 + place_s
-        pos2 = jnp.where(via == me, here * HOP1 + place, -1)
-        hi2, lo2 = extract(pos2, N_CENTER * HOP1, target)
-        out_ref[ROW_D2 + 4 * lev : ROW_D2 + 4 * lev + 4, :] = (hi2 - 1) * base + lo2
+            idx[ROW_POS + k : ROW_POS + k + 1, :] = (via * HOME + (order >> 3))[:, k * LANES : (k + 1) * LANES]
+    via_s, place_s = extract(local, SLOTS, [via + 1, place])
+    idx[ROW_D1 + 4 * lev : ROW_D1 + 4 * lev + 4, :] = (via_s - 1) * HOP1 + place_s
+    pos2 = jnp.where(via == me, here * HOP1 + place, -1)
+    hi2, lo2 = extract(pos2, N_CENTER * HOP1, target)
+    idx[ROW_D2 + 4 * lev : ROW_D2 + 4 * lev + 4, :] = (hi2 - 1) * base + lo2
 
 
 CHUNKS = 2
@@ -120,10 +111,10 @@
 
 
 def main_kernel(
-    idx_ref, emb_ref, cb_ref, books_ref, final_ref,
-    cb, meta_s, meta_r, dsend, drecv, rsend, rrecv, book, h1s, h1r, h2s, h2r, frecv, scatter, member, members, total,
+    codes_hbm, emb_hbm, cb_ref, books_ref, final_ref,
+    codes_ref, emb, idx_ref, cb, meta_s, meta_r, dsend, drecv, rsend, rrecv, book, h1s, h1r, h2s, h2r, frecv, scatter, member, members, total,
     sel1, sel2, sel3,
-    cb_sem, meta_ss, meta_rs, d_ss, d_rs, r_ss, r_rs, g_ss, g_rs, p_rs, h1_ss, h1_rs, h2_ss, h2_rs, f_ss, f_rs, out_sem,
+    codes_sem, emb_sem, cb_sem, meta_ss, meta_rs, d_ss, d_rs, r_ss, r_rs, g_ss, g_rs, p_rs, h1_ss, h1_rs, h2_ss, h2_rs, f_ss, f_rs, out_sem,
 ):
     item, center = lax.axis_index("item"), lax.axis_index("center")
     my_y, my_x, my_c = item // 4, (item // 2) % 2, item % 2
@@ -138,6 +129,10 @@
     def rows(start, size, step):
         return pl.ds(pl.multiple_of(start * step, step), size)
 
+    own_codes = pltpu.make_async_copy(codes_hbm, codes_ref, codes_sem)
+    own_codes.start()
+    own_emb = pltpu.make_async_copy(emb_hbm, emb, emb_sem)
+    own_emb.start()
     barrier = pltpu.get_barrier_semaphore()
     for o in ITEM_OFFSETS:
         pl.semaphore_signal(barrier, inc=1, device_id=(item_at(*o), center), device_id_type=MESH)
@@ -162,14 +157,27 @@
 
     pending = []
 
-    meta_s[...] = jnp.zeros_like(meta_s)
-    for h in range(4):
+    own_codes.wait()
+    known = [slots_of(codes_ref, 0, center)]
+    for k in range(ITEMS // LANES):
+        row = known[0][2][:, k * LANES : (k + 1) * LANES]
+        scatter[0:SLOTS, k * LANES : (k + 1) * LANES] = onehot(iota((SLOTS, LANES), 0) == row)
+    own_emb.wait()
+
+    def send_metas():
+        for lev in range(1, LEVELS):
+            known.append(slots_of(codes_ref, lev, center))
         for lev in range(LEVELS):
-            meta_s[h, lev : lev + 1, :] = idx_ref[ROW_OFF + 4 * lev + h : ROW_OFF + 4 * lev + h + 1, :]
-
-    for k in range(ITEMS // LANES):
-        row = idx_ref[ROW_SLOT0 + k : ROW_SLOT0 + k + 1, :]
-        scatter[0:SLOTS, k * LANES : (k + 1) * LANES] = onehot(iota((SLOTS, LANES), 0) == row)
+            prepare_codes(idx_ref, lev, *known[lev][1:])
+        meta_s[...] = jnp.zeros_like(meta_s)
+        for h in range(4):
+            for lev in range(LEVELS):
+                meta_s[h, lev : lev + 1, :] = idx_ref[ROW_OFF + 4 * lev + h : ROW_OFF + 4 * lev + h + 1, :]
+        for o in ITEM_OFFSETS:
+            to = item_at(*o)
+            send(meta_s.at[to // 4], meta_r.at[item], meta_ss, meta_rs, (to, center))
+        meta_r[item] = meta_s[item // 4]
+        pending.append(whole(meta_r.at[pl.ds(0, 15)], meta_ss, meta_rs))
 
     def selection(ref, first, n_in, n_out):
         for k in range(n_in // LANES):
@@ -199,6 +207,8 @@
             total[lev] = jnp.broadcast_to(count + 1.0, (SHARE, LANES))
 
     def build_selections(lev):
+        nxt = known[min(lev + 1, LEVELS - 1)]
+        prepare_moves(idx_ref, lev, center, known[lev][0], known[lev][2], nxt[0], nxt[2])
         selection(sel1.at[lev], ROW_D1 + 4 * lev, SLOTS, N_CENTER * HOP1)
         selection(sel2.at[lev], ROW_D2 + 4 * lev, N_CENTER * HOP1, N_CENTER * HOP2 if lev < LEVELS - 1 else HOME)
         if lev < LEVELS - 1:
@@ -304,18 +314,15 @@
         def step():
             background[:] = [g for g in background if next(g, 0) is None]
 
-        dsend[0, k] = dot(scatter[0:SLOTS, :], emb_ref[:, cols]).astype(BF16)
+        dsend[0, k] = dot(scatter[0:SLOTS, :], emb[:, cols]).astype(BF16)
         if k == 0:
             pl.semaphore_wait(barrier, len(ITEM_OFFSETS) + len(CENTER_OFFSETS))
-            for o in ITEM_OFFSETS:
-                to = item_at(*o)
-                send(meta_s.at[to // 4], meta_r.at[item], meta_ss, meta_rs, (to, center))
-            meta_r[item] = meta_s[item // 4]
-            pending.append(whole(meta_r.at[pl.ds(0, 15)], meta_ss, meta_rs))
         for lev in range(LEVELS):
             arrived = swap(dsend.at[lev, k], drecv.at[lev, k], d_ss.at[lev, k], d_rs.at[lev, k])
             step()
             if last:
+                if lev == 0:
+                    send_metas()
                 build_selections(lev)
             yield
             if lev == 0 and k == 0:
@@ -370,48 +377,30 @@
         cp.wait_send()
 
 
-PART = 512
-PARTS = (LEVELS + 1) * (ITEMS // PART)
-
-
-def copy_kernel(a_ref, b_ref, oa_ref, ob_ref, hold, in_sem, out_sem):
-    pairs = []
-    for t in range(ITEMS // PART):
-        part = pl.ds(t * PART, PART)
-        pairs += [(a_ref.at[lev, part], oa_ref.at[lev, part]) for lev in range(LEVELS)] + [(b_ref.at[part], ob_ref.at[part])]
-    ins = [pltpu.make_async_copy(src, hold.at[n], in_sem.at[n]) for n, (src, _) in enumerate(pairs)]
-    outs = [pltpu.make_async_copy(hold.at[n], dst, out_sem.at[n]) for n, (_, dst) in enumerate(pairs)]
-    for cp in ins:
+def copy_kernel(a_ref, b_ref, oa_ref, ob_ref, sem):
+    pairs = [(b_ref, ob_ref)] + [(a_ref.at[lev], oa_ref.at[lev]) for lev in range(LEVELS)]
+    cps = [pltpu.make_async_copy(src, dst, sem.at[n]) for n, (src, dst) in enumerate(pairs)]
+    for cp in cps:
         cp.start()
-    for i, o in zip(ins, outs):
-        i.wait()
-        o.start()
-    for cp in outs:
+    for cp in cps:
         cp.wait()
 
 
 def per_device(embeddings, codes, codebooks):
     vmem = pl.BlockSpec(memory_space=pltpu.VMEM)
     hbm = pl.BlockSpec(memory_space=pl.ANY)
-    idx = pl.pallas_call(
-        prep_kernel,
-        out_shape=jax.ShapeDtypeStruct((ROWS, LANES), I32),
-        in_specs=[vmem],
-        out_specs=vmem,
-        compiler_params=pltpu.CompilerParams(vmem_limit_bytes=48 << 20),
-    )(codes)
     dma = pltpu.SemaphoreType.DMA
-    outs = (
-        jax.ShapeDtypeStruct(codebooks.shape, BF16),
-        jax.ShapeDtypeStruct(embeddings.shape, BF16),
-    )
     by_chunk = (LEVELS, CHUNKS)
+    by_block = (LEVELS, N_ITEM // 2, 2, SHARE, DIM)
     books, final = pl.pallas_call(
         main_kernel,
-        out_shape=(jax.ShapeDtypeStruct((LEVELS, N_ITEM // 2, 2, SHARE, DIM), BF16), outs[1]),
-        in_specs=[vmem, vmem, hbm],
-        out_specs=(hbm, vmem),
+        out_shape=(pltpu.VMEM(by_block, BF16), pltpu.VMEM(embeddings.shape, BF16)),
+        in_specs=[hbm, hbm, hbm],
+        out_specs=(vmem, vmem),
         scratch_shapes=[
+            pltpu.VMEM(codes.shape, I32),
+            pltpu.VMEM(embeddings.shape, BF16),
+            pltpu.VMEM((ROWS, LANES), I32),
             pltpu.VMEM((LEVELS, SHARE, DIM), BF16),
             pltpu.VMEM((4, 8, LANES), I32),
             pltpu.VMEM((N_ITEM, 8, LANES), I32),
@@ -432,7 +421,7 @@
             pltpu.VMEM((LEVELS, N_CENTER * HOP1, SLOTS), BF16),
             pltpu.VMEM((LEVELS, N_CENTER * HOP2, N_CENTER * HOP1), BF16),
             pltpu.VMEM((LEVELS - 1, SLOTS, N_CENTER * HOP2), BF16),
-            dma,
+            dma, dma, dma,
             dma, dma,
             dma(by_chunk), dma(by_chunk),
             dma(by_chunk), dma(by_chunk),
@@ -442,16 +431,17 @@
             dma((CHUNKS,)), dma((CHUNKS, 9)),
             dma(by_chunk),
         ],
-        compiler_params=pltpu.CompilerParams(collective_id=0, has_side_effects=True, vmem_limit_bytes=60 << 20),
-    )(idx, embeddings, codebooks)
-    return pl.pallas_call(
+        compiler_params=pltpu.CompilerParams(collective_id=0, has_side_effects=True, vmem_limit_bytes=48 << 20),
+    )(codes, embeddings, codebooks)
+    books, final = pl.pallas_call(
         copy_kernel,
-        out_shape=outs,
-        in_specs=[hbm, hbm],
+        out_shape=(jax.ShapeDtypeStruct(by_block, BF16), jax.ShapeDtypeStruct(embeddings.shape, BF16)),
+        in_specs=[vmem, vmem],
         out_specs=(hbm, hbm),
-        scratch_shapes=[pltpu.VMEM((PARTS, PART, DIM), BF16), dma((PARTS,)), dma((PARTS,))],
-        compiler_params=pltpu.CompilerParams(vmem_limit_bytes=60 << 20),
-    )(books.reshape(codebooks.shape), final)
+        scratch_shapes=[dma((LEVELS + 1,))],
+        compiler_params=pltpu.CompilerParams(vmem_limit_bytes=4 << 20),
+    )(books, final)
+    return books.reshape(codebooks.shape), final
 
 
 def solution(mesh):

time: 127 us -> 119 us (0.937)
  Pallas kernels: 125 us -> 118 us
  local copies, waits for them, and re-layouts: 1.39 us -> 0 us
    pallas_call x3 -> x2, Pallas kernels: 125 us -> 118 us  [the longest x1 114 us: per_device(): pl.pallas_call(main_kernel, out_shape=(pltpu.VMEM(by_block, BF16), pltpu....]
    unnamed x4 -> x0, local copies, waits for them, and re-layouts: 1.39 us -> none
where the time goes in v4:
time: 119 us
  Pallas kernels  118 us (99%)
    pallas_call x1, Pallas kernels, per_device(): pl.pallas_call(main_kernel, out_shape=(pltpu.VMEM(by_block, BF16), pltpu....  114 us
    pallas_call x1, Pallas kernels, per_device(): pl.pallas_call(copy_kernel, out_shape=(jax.ShapeDtypeStruct(by_block, BF1...  3.37 us

profile of v4, /device:TPU:0, one launch (start us, length us, event | category | flops | bytes accessed | tf_op | source)
XLA Modules:
  0.0 118.6 jit_solution(8244856863858416348)
XLA Ops:
  0.6 114.4 %shard_map.50 = (bf16[3,8,2,128,512]{4,3,2,1,0:T(8,128)(2,1)S(1)}, bf16[2048,512]{1,0:T(8,128)(2,1)S(1)}) custom-call(s32[3,2048]{1,0:T(4,128)} %codes_hbm.1, bf16[2048,512]{1,0:T(8,128)(2,1)} %emb_hbm.1, bf16[3,2048,512]{2,1,0:T(8,128)(2,1)} %cb_ref.1), custom_call_target="tpu_custom_call" | custom-call | tf_op jit(solution)/shard_map/pallas_call | solution.py:395
  115.1 3.4 %shard_map.51 = (bf16[3,8,2,128,512]{4,3,2,1,0:T(8,128)(2,1)}, bf16[2048,512]{1,0:T(8,128)(2,1)}) custom-call(bf16[3,8,2,128,512]{4,3,2,1,0:T(8,128)(2,1)S(1)} %get-tuple-element.6.a_ref, bf16[2048,512]{1,0:T(8,128)(2,1)S(1)} %get-tuple-element.7.b_ref), custom_call_target="tpu_custom_call" | custom-call | tf_op jit(solution)/shard_map/pallas_call | solution.py:436

commit v5 on v4

--- a/solution.py
+++ b/solution.py
@@ -34,6 +34,9 @@
 ROW_D3 = 36
 ROW_POS = 48
 ROWS = 64
+
+
+ARRIVALS = [(0, 0), (3, 0), (1, 0), (0, 1), (3, 1), (1, 1), (2, 0), (2, 1)]
 
 
 def ordered(cls, n_cls, lower=None):
@@ -95,8 +98,12 @@
         via, place = order & 7, rank >> 3
         target = [jnp.ones_like(order), order >> 3]
         base = HOME
+        z, h = (via - me) & 3, (via >> 2) != me // 4
+        arrival = jnp.zeros_like(via)
+        for n, (dz, dh) in enumerate(ARRIVALS):
+            arrival = jnp.where((z == dz) & (h == (dh == 1)), n, arrival)
         for k in range(ITEMS // LANES):
-            idx[ROW_POS + k : ROW_POS + k + 1, :] = (via * HOME + (order >> 3))[:, k * LANES : (k + 1) * LANES]
+            idx[ROW_POS + k : ROW_POS + k + 1, :] = (arrival * HOME + (order >> 3))[:, k * LANES : (k + 1) * LANES]
     via_s, place_s = extract(local, SLOTS, [via + 1, place])
     idx[ROW_D1 + 4 * lev : ROW_D1 + 4 * lev + 4, :] = (via_s - 1) * HOP1 + place_s
     pos2 = jnp.where(via == me, here * HOP1 + place, -1)
@@ -106,8 +113,8 @@
 
 CHUNKS = 2
 WIDTH = DIM // CHUNKS
-ITEM_OFFSETS = [(y, x, c) for y in range(4) for x in range(2) for c in range(2)][1:]
-CENTER_OFFSETS = [(h, z) for h in range(2) for z in range(4)][1:]
+ITEM_OFFSETS = sorted([(y, x, c) for y in range(4) for x in range(2) for c in range(2)][1:], key=lambda o: -(4 * o[1] + min(o[0], 4 - o[0])))
+CENTER_OFFSETS = sorted([(h, z) for h in range(2) for z in range(4)][1:], key=lambda o: -(2 * o[0] + min(o[1], 4 - o[1])))
 
 
 def main_kernel(
@@ -206,16 +213,21 @@
             count = jnp.sum(member[lev].astype(F32), axis=1, keepdims=True)
             total[lev] = jnp.broadcast_to(count + 1.0, (SHARE, LANES))
 
-    def build_selections(lev):
+    def moves(lev):
         nxt = known[min(lev + 1, LEVELS - 1)]
         prepare_moves(idx_ref, lev, center, known[lev][0], known[lev][2], nxt[0], nxt[2])
+
+    def first_selection(lev):
         selection(sel1.at[lev], ROW_D1 + 4 * lev, SLOTS, N_CENTER * HOP1)
+
+    def second_selection(lev):
         selection(sel2.at[lev], ROW_D2 + 4 * lev, N_CENTER * HOP1, N_CENTER * HOP2 if lev < LEVELS - 1 else HOME)
-        if lev < LEVELS - 1:
-            selection(sel3.at[lev], ROW_D3 + 6 * lev, N_CENTER * HOP2, SLOTS)
-
-    def build_scatter():
-        for k in range(ITEMS // LANES):
+
+    def third_selection(lev):
+        selection(sel3.at[lev], ROW_D3 + 6 * lev, N_CENTER * HOP2, SLOTS)
+
+    def build_scatter(n):
+        for k in range(3 * n, min(3 * n + 3, ITEMS // LANES)):
             row = jnp.broadcast_to(idx_ref[ROW_POS + k : ROW_POS + k + 1, :].astype(F32), (LANES, LANES))
             col = row.T.astype(I32)
             for g in range(ITEMS // LANES):
@@ -296,6 +308,14 @@
         pending.append(cp)
         return cp
 
+    def place(k, cols, part):
+        blocks = [frecv[k, rows(center_at(h, z), HOME, HOME), :] for z, h in ARRIVALS[4 * part : 4 * part + 4]]
+        source = jnp.concatenate(blocks, axis=0)
+        for t in range(ITEMS // 256):
+            at = slice(t * 256, (t + 1) * 256)
+            found = dot(scatter[at, 4 * part * HOME : 4 * (part + 1) * HOME], source).astype(BF16)
+            final_ref[at, cols] = found if part == 0 else final_ref[at, cols] + found
+
     def swap(src, dst, ss, rs):
         own_rows = rows(item, CAP, CAP)
         for o in ITEM_OFFSETS:
@@ -306,10 +326,35 @@
         pending.append(cp)
         return cp
 
+    def do(f, *args):
+        return lambda: f(*args)
+
+    chores = [
+        [send_metas, do(moves, 0)],
+        [do(first_selection, 0), do(second_selection, 0)],
+        [do(third_selection, 0), do(moves, 1)],
+        [do(first_selection, 1), do(second_selection, 1)],
+        [do(third_selection, 1)],
+        [do(moves, 2)],
+        [do(first_selection, 2), do(second_selection, 2)],
+        [do(build_scatter, 0)],
+        [do(build_scatter, 1)],
+        [do(build_scatter, 2)],
+        [do(build_scatter, 3)],
+        [do(build_scatter, 4)],
+        [do(build_scatter, 5)],
+        [],
+    ]
+
     def program(k):
         cols = slice(k * WIDTH, (k + 1) * WIDTH)
         last = k == CHUNKS - 1
         background = []
+
+        def idle():
+            if last:
+                for chore in chores.pop(0):
+                    chore()
 
         def step():
             background[:] = [g for g in background if next(g, 0) is None]
@@ -320,10 +365,7 @@
         for lev in range(LEVELS):
             arrived = swap(dsend.at[lev, k], drecv.at[lev, k], d_ss.at[lev, k], d_rs.at[lev, k])
             step()
-            if last:
-                if lev == 0:
-                    send_metas()
-                build_selections(lev)
+            idle()
             yield
             if lev == 0 and k == 0:
                 receive_metas()
@@ -335,36 +377,41 @@
             arrived = swap(rsend.at[lev, k], rrecv.at[lev, k], r_ss.at[lev, k], r_rs.at[lev, k])
             book[lev, k, rows(my_c * 8 + item // 2, SHARE, SHARE), :] = updated
             step()
-            background.append(gather_books(lev, k))
-            next(background[-1])
+            fresh = gather_books(lev, k)
+            idle()
             yield
             arrived.wait_recv()
             h1s[lev, k] = select(sel1.at[lev], SLOTS, N_CENTER * HOP1, rrecv[lev, k])
             hop = exchange(h1s.at[lev, k], h1r.at[lev, k], HOP1, h1_ss.at[lev, k], h1_rs.at[lev, k])
             step()
-            if last and lev == LEVELS - 1:
-                build_scatter()
+            background.append(fresh)
+            next(fresh)
+            idle()
             yield
             hop.wait_recv()
             if lev < LEVELS - 1:
                 h2s[lev, k] = select(sel2.at[lev], N_CENTER * HOP1, N_CENTER * HOP2, h1r[lev, k])
                 hop = exchange(h2s.at[lev, k], h2r.at[lev, k], HOP2, h2_ss.at[lev, k], h2_rs.at[lev, k])
                 step()
+                idle()
                 yield
                 hop.wait_recv()
                 dsend[lev + 1, k] = select(sel3.at[lev], N_CENTER * HOP2, SLOTS, h2r[lev, k])
             else:
                 frecv[k, rows(center, HOME, HOME), :] = select(sel2.at[lev], N_CENTER * HOP1, HOME, h1r[lev, k])
-                for _ in gather_rows(k):
+                phases = gather_rows(k)
+                for phase in range(3):
+                    next(phases)
                     step()
+                    idle()
+                    if phase == 2:
+                        place(k, cols, 0)
                     yield
+                next(phases, 0)
                 while background:
                     step()
+                place(k, cols, 1)
                 pending.append(whole(frecv.at[k, pl.ds(0, 7 * HOME)], f_ss.at[k], f_rs.at[k, 0]))
-                for t in range(ITEMS // 256):
-                    final_ref[t * 256 : (t + 1) * 256, cols] = dot(
-                        scatter[t * 256 : (t + 1) * 256, :], frecv[k]
-                    ).astype(BF16)
 
     running = [program(k) for k in range(CHUNKS)]
     while running:
@@ -378,7 +425,8 @@
 
 
 def copy_kernel(a_ref, b_ref, oa_ref, ob_ref, sem):
-    pairs = [(b_ref, ob_ref)] + [(a_ref.at[lev], oa_ref.at[lev]) for lev in range(LEVELS)]
+    pairs = [(b_ref.at[pl.ds(h * 512, 512)], ob_ref.at[pl.ds(h * 512, 512)]) for h in range(4)]
+    pairs += [(a_ref.at[lev, q], oa_ref.at[lev, q]) for lev in range(LEVELS) for q in range(N_ITEM // 2)]
     cps = [pltpu.make_async_copy(src, dst, sem.at[n]) for n, (src, dst) in enumerate(pairs)]
     for cp in cps:
         cp.start()
@@ -438,7 +486,7 @@
         out_shape=(jax.ShapeDtypeStruct(by_block, BF16), jax.ShapeDtypeStruct(embeddings.shape, BF16)),
         in_specs=[vmem, vmem],
         out_specs=(hbm, hbm),
-        scratch_shapes=[dma((LEVELS + 1,))],
+        scratch_shapes=[dma((4 + LEVELS * N_ITEM // 2,))],
         compiler_params=pltpu.CompilerParams(vmem_limit_bytes=4 << 20),
     )(books, final)
     return books.reshape(codebooks.shape), final

time: 119 us -> 116 us (0.975)
  Pallas kernels: 118 us -> 114 us
    pallas_call x1, Pallas kernels: 114 us -> 111 us  [per_device(): pl.pallas_call(main_kernel, out_shape=(pltpu.VMEM(by_block, BF16), pltpu....]
where the time goes in v5:
time: 116 us; the launch traced here: 115 us
  Pallas kernels  114 us (98%)
    pallas_call x1, Pallas kernels, per_device(): pl.pallas_call(main_kernel, out_shape=(pltpu.VMEM(by_block, BF16), pltpu....  111 us
    pallas_call x1, Pallas kernels, per_device(): pl.pallas_call(copy_kernel, out_shape=(jax.ShapeDtypeStruct(by_block, BF1...  3.51 us

profile of v5, /device:TPU:0, one launch (start us, length us, event | category | flops | bytes accessed | tf_op | source)
XLA Modules:
  0.0 115.2 jit_solution(4962875803007883763)
XLA Ops:
  0.6 110.9 %shard_map.50 = (bf16[3,8,2,128,512]{4,3,2,1,0:T(8,128)(2,1)S(1)}, bf16[2048,512]{1,0:T(8,128)(2,1)S(1)}) custom-call(s32[3,2048]{1,0:T(4,128)} %codes_hbm.1, bf16[2048,512]{1,0:T(8,128)(2,1)} %emb_hbm.1, bf16[3,2048,512]{2,1,0:T(8,128)(2,1)} %cb_ref.1), custom_call_target="tpu_custom_call" | custom-call | tf_op jit(solution)/shard_map/pallas_call | solution.py:443
  111.5 3.5 %shard_map.51 = (bf16[3,8,2,128,512]{4,3,2,1,0:T(8,128)(2,1)}, bf16[2048,512]{1,0:T(8,128)(2,1)}) custom-call(bf16[3,8,2,128,512]{4,3,2,1,0:T(8,128)(2,1)S(1)} %get-tuple-element.6.a_ref, bf16[2048,512]{1,0:T(8,128)(2,1)S(1)} %get-tuple-element.7.b_ref), custom_call_target="tpu_custom_call" | custom-call | tf_op jit(solution)/shard_map/pallas_call | solution.py:484

commit v6 on v5

--- a/solution.py
+++ b/solution.py
@@ -112,6 +112,7 @@
 
 
 CHUNKS = 2
+TILE = 64
 WIDTH = DIM // CHUNKS
 ITEM_OFFSETS = sorted([(y, x, c) for y in range(4) for x in range(2) for c in range(2)][1:], key=lambda o: -(4 * o[1] + min(o[0], 4 - o[0])))
 CENTER_OFFSETS = sorted([(h, z) for h in range(2) for z in range(4)][1:], key=lambda o: -(2 * o[0] + min(o[1], 4 - o[1])))
@@ -167,8 +168,16 @@
     own_codes.wait()
     known = [slots_of(codes_ref, 0, center)]
     for k in range(ITEMS // LANES):
-        row = known[0][2][:, k * LANES : (k + 1) * LANES]
-        scatter[0:SLOTS, k * LANES : (k + 1) * LANES] = onehot(iota((SLOTS, LANES), 0) == row)
+        idx_ref[ROW_POS + k : ROW_POS + k + 1, :] = known[0][2][:, k * LANES : (k + 1) * LANES]
+
+    @pl.loop(0, SLOTS // TILE)
+    def _(t):
+        at = pl.multiple_of(t * TILE, TILE)
+        for k in range(ITEMS // LANES):
+            scatter[pl.ds(at, TILE), k * LANES : (k + 1) * LANES] = onehot(
+                iota((TILE, LANES), 0) + at == idx_ref[ROW_POS + k : ROW_POS + k + 1, :]
+            )
+
     own_emb.wait()
 
     def send_metas():
@@ -187,10 +196,13 @@
         pending.append(whole(meta_r.at[pl.ds(0, 15)], meta_ss, meta_rs))
 
     def selection(ref, first, n_in, n_out):
-        for k in range(n_in // LANES):
-            ref[0:n_out, k * LANES : (k + 1) * LANES] = onehot(
-                iota((n_out, LANES), 0) == idx_ref[first + k : first + k + 1, :]
-            )
+        @pl.loop(0, n_out // TILE)
+        def _(t):
+            at = pl.multiple_of(t * TILE, TILE)
+            for k in range(n_in // LANES):
+                ref[pl.ds(at, TILE), k * LANES : (k + 1) * LANES] = onehot(
+                    iota((TILE, LANES), 0) + at == idx_ref[first + k : first + k + 1, :]
+                )
 
     def select(ref, n_in, n_out, source):
         return dot(ref[0:n_out, 0:n_in], source).astype(BF16)
@@ -227,13 +239,13 @@
         selection(sel3.at[lev], ROW_D3 + 6 * lev, N_CENTER * HOP2, SLOTS)
 
     def build_scatter(n):
-        for k in range(3 * n, min(3 * n + 3, ITEMS // LANES)):
-            row = jnp.broadcast_to(idx_ref[ROW_POS + k : ROW_POS + k + 1, :].astype(F32), (LANES, LANES))
+        @pl.loop(3 * n, min(3 * n + 3, ITEMS // LANES))
+        def _(k):
+            row = jnp.broadcast_to(idx_ref[pl.ds(ROW_POS + k, 1), :].astype(F32), (LANES, LANES))
             col = row.T.astype(I32)
+            at = pl.ds(pl.multiple_of(k * LANES, LANES), LANES)
             for g in range(ITEMS // LANES):
-                scatter[k * LANES : (k + 1) * LANES, g * LANES : (g + 1) * LANES] = onehot(
-                    iota((LANES, LANES), 1) + g * LANES == col
-                )
+                scatter[at, g * LANES : (g + 1) * LANES] = onehot(iota((LANES, LANES), 1) + g * LANES == col)
 
     def mover(buf, size, ring, ss, rs):
         def move(n, at, to, part=None):

time: 116 us -> 115 us (level)
  no operation moved by 1% of the time
where the time goes in v6:
time: 115 us; the launch traced here: 114 us
  Pallas kernels  113 us (98%)
    pallas_call x1, Pallas kernels, per_device(): pl.pallas_call(main_kernel, out_shape=(pltpu.VMEM(by_block, BF16), pltpu....  110 us
    pallas_call x1, Pallas kernels, per_device(): pl.pallas_call(copy_kernel, out_shape=(jax.ShapeDtypeStruct(by_block, BF1...  3.51 us

profile of v6, /device:TPU:0, one launch (start us, length us, event | category | flops | bytes accessed | tf_op | source)
XLA Modules:
  0.0 114.2 jit_solution(12301525850572233785)
XLA Ops:
  0.6 109.9 %shard_map.50 = (bf16[3,8,2,128,512]{4,3,2,1,0:T(8,128)(2,1)S(1)}, bf16[2048,512]{1,0:T(8,128)(2,1)S(1)}) custom-call(s32[3,2048]{1,0:T(4,128)} %codes_hbm.1, bf16[2048,512]{1,0:T(8,128)(2,1)} %emb_hbm.1, bf16[3,2048,512]{2,1,0:T(8,128)(2,1)} %cb_ref.1), custom_call_target="tpu_custom_call" | custom-call | tf_op jit(solution)/shard_map/pallas_call | solution.py:455
  110.5 3.5 %shard_map.51 = (bf16[3,8,2,128,512]{4,3,2,1,0:T(8,128)(2,1)}, bf16[2048,512]{1,0:T(8,128)(2,1)}) custom-call(bf16[3,8,2,128,512]{4,3,2,1,0:T(8,128)(2,1)S(1)} %get-tuple-element.6.a_ref, bf16[2048,512]{1,0:T(8,128)(2,1)S(1)} %get-tuple-element.7.b_ref), custom_call_target="tpu_custom_call" | custom-call | tf_op jit(solution)/shard_map/pallas_call | solution.py:496

commit v7 on v6

--- a/solution.py
+++ b/solution.py
@@ -70,10 +70,10 @@
 
 def slots_of(codes_ref, lev, me):
     code = codes_ref[lev : lev + 1, :]
-    block = code >> 7
-    rank, _ = ordered(block, N_ITEM * N_CENTER)
     shard = code >> 11
-    return shard, code & (SHARE - 1), jnp.where(shard == me, (block & (N_ITEM - 1)) * CAP + rank, -1)
+    block = jnp.where(shard == me, (code >> 7) & (N_ITEM - 1), -1)
+    rank, _ = ordered(block, N_ITEM)
+    return shard, code & (SHARE - 1), jnp.where(shard == me, block * CAP + rank, -1)
 
 
 def prepare_codes(idx, lev, off, local):
@@ -276,7 +276,10 @@
         d.wait_recv()
         rest.append(move(8, (2, 0), over, 1))
         yield
-        for cp in rest:
+        for cp in rest[:2]:
+            cp.wait_recv()
+        yield
+        for cp in rest[2:]:
             cp.wait_recv()
 
     def gather_books(lev, k):
@@ -320,13 +323,13 @@
         pending.append(cp)
         return cp
 
-    def place(k, cols, part):
-        blocks = [frecv[k, rows(center_at(h, z), HOME, HOME), :] for z, h in ARRIVALS[4 * part : 4 * part + 4]]
+    def place(k, cols, first, stop):
+        blocks = [frecv[k, rows(center_at(h, z), HOME, HOME), :] for z, h in ARRIVALS[first:stop]]
         source = jnp.concatenate(blocks, axis=0)
         for t in range(ITEMS // 256):
             at = slice(t * 256, (t + 1) * 256)
-            found = dot(scatter[at, 4 * part * HOME : 4 * (part + 1) * HOME], source).astype(BF16)
-            final_ref[at, cols] = found if part == 0 else final_ref[at, cols] + found
+            found = dot(scatter[at, first * HOME : stop * HOME], source).astype(BF16)
+            final_ref[at, cols] = found if first == 0 else final_ref[at, cols] + found
 
     def swap(src, dst, ss, rs):
         own_rows = rows(item, CAP, CAP)
@@ -417,12 +420,14 @@
                     step()
                     idle()
                     if phase == 2:
-                        place(k, cols, 0)
+                        place(k, cols, 0, 4)
                     yield
+                next(phases)
+                place(k, cols, 4, 7)
                 next(phases, 0)
                 while background:
                     step()
-                place(k, cols, 1)
+                place(k, cols, 7, 8)
                 pending.append(whole(frecv.at[k, pl.ds(0, 7 * HOME)], f_ss.at[k], f_rs.at[k, 0]))
 
     running = [program(k) for k in range(CHUNKS)]

time: 115 us -> 113 us (0.983); the launches traced: 114 us -> 113 us
  no operation moved by 1% of the time
where the time goes in v7:
time: 113 us
  Pallas kernels  113 us (100%)
    pallas_call x1, Pallas kernels, per_device(): pl.pallas_call(main_kernel, out_shape=(pltpu.VMEM(by_block, BF16), pltpu....  109 us
    pallas_call x1, Pallas kernels, per_device(): pl.pallas_call(copy_kernel, out_shape=(jax.ShapeDtypeStruct(by_block, BF1...  3.51 us

profile of v7, /device:TPU:0, one launch (start us, length us, event | category | flops | bytes accessed | tf_op | source)
XLA Modules:
  0.0 113.3 jit_solution(8785378810245389710)
XLA Ops:
  0.6 109.0 %shard_map.50 = (bf16[3,8,2,128,512]{4,3,2,1,0:T(8,128)(2,1)S(1)}, bf16[2048,512]{1,0:T(8,128)(2,1)S(1)}) custom-call(s32[3,2048]{1,0:T(4,128)} %codes_hbm.1, bf16[2048,512]{1,0:T(8,128)(2,1)} %emb_hbm.1, bf16[3,2048,512]{2,1,0:T(8,128)(2,1)} %cb_ref.1), custom_call_target="tpu_custom_call" | custom-call | tf_op jit(solution)/shard_map/pallas_call | solution.py:460
  109.7 3.5 %shard_map.51 = (bf16[3,8,2,128,512]{4,3,2,1,0:T(8,128)(2,1)}, bf16[2048,512]{1,0:T(8,128)(2,1)}) custom-call(bf16[3,8,2,128,512]{4,3,2,1,0:T(8,128)(2,1)S(1)} %get-tuple-element.6.a_ref, bf16[2048,512]{1,0:T(8,128)(2,1)S(1)} %get-tuple-element.7.b_ref), custom_call_target="tpu_custom_call" | custom-call | tf_op jit(solution)/shard_map/pallas_call | solution.py:501

commit v8 on v7

--- a/solution.py
+++ b/solution.py
@@ -393,14 +393,18 @@
             book[lev, k, rows(my_c * 8 + item // 2, SHARE, SHARE), :] = updated
             step()
             fresh = gather_books(lev, k)
+            if lev == LEVELS - 1:
+                background.append(fresh)
+                next(fresh)
             idle()
             yield
             arrived.wait_recv()
             h1s[lev, k] = select(sel1.at[lev], SLOTS, N_CENTER * HOP1, rrecv[lev, k])
             hop = exchange(h1s.at[lev, k], h1r.at[lev, k], HOP1, h1_ss.at[lev, k], h1_rs.at[lev, k])
             step()
-            background.append(fresh)
-            next(fresh)
+            if lev < LEVELS - 1:
+                background.append(fresh)
+                next(fresh)
             idle()
             yield
             hop.wait_recv()

time: 113 us -> 114 us (level)
  no operation moved by 1% of the time
where the time goes in v8:
time: 114 us
  Pallas kernels  113 us (99%)
    pallas_call x1, Pallas kernels, per_device(): pl.pallas_call(main_kernel, out_shape=(pltpu.VMEM(by_block, BF16), pltpu....  110 us
    pallas_call x1, Pallas kernels, per_device(): pl.pallas_call(copy_kernel, out_shape=(jax.ShapeDtypeStruct(by_block, BF1...  3.51 us

profile of v8, /device:TPU:0, one launch (start us, length us, event | category | flops | bytes accessed | tf_op | source)
XLA Modules:
  0.0 113.9 jit_solution(6537933686782413529)
XLA Ops:
  0.6 109.6 %shard_map.50 = (bf16[3,8,2,128,512]{4,3,2,1,0:T(8,128)(2,1)S(1)}, bf16[2048,512]{1,0:T(8,128)(2,1)S(1)}) custom-call(s32[3,2048]{1,0:T(4,128)} %codes_hbm.1, bf16[2048,512]{1,0:T(8,128)(2,1)} %emb_hbm.1, bf16[3,2048,512]{2,1,0:T(8,128)(2,1)} %cb_ref.1), custom_call_target="tpu_custom_call" | custom-call | tf_op jit(solution)/shard_map/pallas_call | solution.py:464
  110.2 3.5 %shard_map.51 = (bf16[3,8,2,128,512]{4,3,2,1,0:T(8,128)(2,1)}, bf16[2048,512]{1,0:T(8,128)(2,1)}) custom-call(bf16[3,8,2,128,512]{4,3,2,1,0:T(8,128)(2,1)S(1)} %get-tuple-element.6.a_ref, bf16[2048,512]{1,0:T(8,128)(2,1)S(1)} %get-tuple-element.7.b_ref), custom_call_target="tpu_custom_call" | custom-call | tf_op jit(solution)/shard_map/pallas_call | solution.py:505
